TPU v7x, 256 devices: a whole 4x4x8 slice. The times are simulated.
256 devices in a mesh: blk: 64 (over x, z, y_lo), narrow: 4 (over y_hi, core).
Axes of the slice: x: 4, y: 4 (y_hi: 2, y_lo: 2; y = y_hi * 2 + y_lo), z: 8, core: 2. Of those that a mesh axis runs over, the one named last changes fastest.
Arguments:
- embed_low: bfloat16 [32768, 384], P(('blk', 'narrow')), may hold values from -0.3125 to 0.3125
- embed_high: bfloat16 [32768, 384], P(('blk', 'narrow')), may hold values from -0.3125 to 0.3125
- partner: int32 [32768], P(('blk', 'narrow')), may hold values from 0 to 32767, each once
- log_scale: float32 [], replicated, may hold values from 3 to 4.1
- bias: float32 [], replicated, may hold values from -6 to -4
Outputs:
- grad_low: float32 [32768, 384], P(('blk', 'narrow'))
- grad_high: float32 [32768, 384], P(('blk', 'narrow'))
Inputs may be any that keep to these rules, and one draw needn't show every extreme that they name: Each 40x crop is the partner of exactly one 10x crop.
All inputs are finite; a program needn't handle non-finite values.
Results may differ from a plain program's by a relative error of at most 0.00065.
Values may be sent and summed in bfloat16 or wider, within the bound.
A program may use at most 64 MiB of HBM per device.

v0:
```python
import jax
import jax.numpy as jnp
from jax import lax
from jax.sharding import PartitionSpec as P


def shortened(shard):

    def short(part):
        return part.astype(jnp.bfloat16) if part.dtype == jnp.float32 else part

    return jax.tree.map(short, shard)


def passed_along(value, axis, steps):
    count = lax.axis_size(axis)
    pairs = [(source, (source + steps) % count) for source in range(count)]
    return lax.ppermute(value, axis, pairs)


def weigh(low_rows, partners, high_rows, first, scale, bias):
    logits = (
        scale
        * lax.dot_general(
            low_rows, high_rows, (((1,), (1,)), ((), ())), preferred_element_type=jnp.float32
        )
        + bias
    )
    columns = first + lax.iota(jnp.int32, high_rows.shape[0])
    match = (partners[:, None] == columns[None, :]).astype(jnp.float32)
    return (scale * (jax.nn.sigmoid(logits) - match)).astype(jnp.bfloat16)


def per_device(embed_low, embed_high, partner, log_scale, bias):
    scale = jnp.exp(log_scale)
    rows = embed_low.shape[0]
    width = embed_low.shape[1]
    high_group = lax.all_gather(embed_high, "narrow", axis=0, tiled=True)
    first = lax.axis_index("blk") * high_group.shape[0]
    stations = lax.axis_size("blk")

    def absorb(bundle, accum, portion):
        low_rows, partners = bundle
        weights = weigh(low_rows, partners, high_group, first, scale, bias)
        accum = accum + jnp.dot(weights, high_group, preferred_element_type=jnp.float32)
        portion = portion + lax.dot_general(
            weights, low_rows, (((0,), (0,)), ((), ())), preferred_element_type=jnp.float32
        )
        return (accum, portion)

    bundles = ((embed_low, partner),)
    accums = (jnp.zeros((rows, width), jnp.float32),)

    def advance(bundles, accums):
        moved = passed_along(shortened(bundles[0]), "blk", 1)
        accum_moved = passed_along(accums[0], "blk", 1)
        return ((moved,), (accum_moved,))

    def visit(bundles, accums, portion):
        updated = []
        for bundle, accum in zip(bundles, accums):
            accum, portion = absorb(bundle, accum, portion)
            updated.append(accum)
        return (tuple(updated), portion)

    def turn(step, carry):
        bundles, accums, portion = carry
        accums, portion = visit(bundles, accums, portion)
        bundles, accums = advance(bundles, accums)
        return (bundles, accums, portion)

    portion = jnp.zeros((high_group.shape[0], width), jnp.float32)
    bundles, accums, portion = lax.fori_loop(0, stations - 1, turn, (bundles, accums, portion))
    accums, portion = visit(bundles, accums, portion)
    grad_low = passed_along(accums[0], "blk", 1)
    grad_high = lax.psum_scatter(portion, "narrow", scatter_dimension=0, tiled=True)
    return (grad_low, grad_high)


def solution(mesh):
    in_specs = (
        P(("blk", "narrow"), None),
        P(("blk", "narrow"), None),
        P(("blk", "narrow")),
        P(),
        P(),
    )
    out_specs = (P(("blk", "narrow"), None), P(("blk", "narrow"), None))
    return jax.shard_map(
        per_device, mesh=mesh, in_specs=in_specs, out_specs=out_specs, check_vma=False
    )
```

profile of v0, /device:TPU:1, one launch (start us, length us, event | category | flops | bytes accessed | tf_op | source)
XLA Modules:
  0.0 837.1 jit_solution(16956113376601377781)
XLA Ops:
  8.1 10.7 %all_gather.3 = bf16[512,384]{1,0:T(8,128)(2,1)S(1)} all-gather(bf16[128,384]{1,0:T(8,128)(2,1)S(1)} %copy-done.1), channel_id=1, replica_groups=mesh['blk'=64,'narrow'=4] {'narrow'}, dimensions={0}, use_global_device_ids=true | all-gather | bytes 491520 | tf_op jit(solution)/shard_map/all_gather | solution.py:38
  21.0 714.6 %while.17 = (s32[]{:T(128)}, bf16[128,384]{1,0:T(8,128)(2,1)S(1)}, s32[128]{0:T(128)S(1)}, f32[128,384]{1,0:T(8,128)S(1)}, f32[512,384]{1,0:T(8,128)S(1)}, /*ind...) while((s32[]{:T(128)}, bf16[128,384]{1,0:T(8,128)(2,1)S(1)}, ...), condition=%wide.region_1.0_spmd.clone, body=%wide.region_0.0_spmd.clone.sunk | while | flops 152093184 | bytes 4726523 | solution.py:73
  25.2 6.0 collective-permute-done.1
  37.0 5.9 collective-permute-done.1
  49.6 5.9 collective-permute-done.1
  73.2 5.9 collective-permute-done.1
  84.2 5.9 collective-permute-done.1
  104.7 5.9 collective-permute-done.1
  125.1 6.2 collective-permute-done.1
  135.4 7.1 collective-permute-done.1
  146.9 7.2 collective-permute-done.1
  159.7 6.4 collective-permute-done.1
  172.2 5.9 collective-permute-done.1
  184.7 5.9 collective-permute-done.1
  196.6 5.9 collective-permute-done.1
  218.8 5.9 collective-permute-done.1
  229.1 5.9 collective-permute-done.1
  259.8 6.4 collective-permute-done.1
  270.1 7.2 collective-permute-done.1
  281.9 7.2 collective-permute-done.1
  294.9 6.4 collective-permute-done.1
  307.5 5.9 collective-permute-done.1
  331.8 5.9 collective-permute-done.1
  354.1 5.9 collective-permute-done.1
  364.3 5.9 collective-permute-done.1
  395.0 6.4 collective-permute-done.1
  405.4 7.2 collective-permute-done.1
  417.1 7.2 collective-permute-done.1
  430.2 6.4 collective-permute-done.1
  442.7 5.9 collective-permute-done.1
  467.1 5.9 collective-permute-done.1
  489.3 5.9 collective-permute-done.1
  499.6 5.9 collective-permute-done.1
  530.3 6.4 collective-permute-done.1
  540.6 7.2 collective-permute-done.1
  552.4 7.2 collective-permute-done.1
  565.4 6.4 collective-permute-done.1
  578.0 5.9 collective-permute-done.1
  602.3 5.9 collective-permute-done.1
  624.6 5.9 collective-permute-done.1
  634.8 5.9 collective-permute-done.1
  665.5 6.4 collective-permute-done.1
  675.8 7.2 collective-permute-done.1
  687.6 7.2 collective-permute-done.1
  700.6 6.4 collective-permute-done.1
  713.2 5.9 collective-permute-done.1
  737.5 10.3 %collective-permute-done.3 = f32[128,384]{1,0:T(8,128)S(1)} collective-permute-done((f32[128,384]{1,0:T(8,128)S(1)}, f32[128,384]{1,0:T(8,128)S(1)}, u32[]{:S(2)}, u32[]{:S(2)}) %collective-permute-start.3) | collective-permute-done | bytes 196640 | tf_op jit(solution)/shard_map/ppermute | solution.py:18
  747.8 81.8 %reduce-scatter.2.cloned.1.call-done = f32[128,384]{1,0:T(8,128)} async-done(((f32[512,384]{1,0:T(8,128)}), f32[128,384]{1,0:T(8,128)}) %reduce-scatter.2.cloned.1.call-update) | async-done | bytes 196624 | tf_op jit(solution)/shard_map/reduce_scatter | solution.py:76
  (728 shorter events, 435.9 us)
Async XLA Ops:
  7.2 822.5 %reduce-scatter.2.cloned.1.call-start = ((), (), s32[]{:S(2)}) async-start(), calls=%async_computation.1 | async-start | bytes 983040 | tf_op jit(solution)/shard_map/reduce_scatter | solution.py:76
  21.0 10.1 %collective-permute-start = (bf16[128,384]{1,0:T(8,128)(2,1)S(1)}, bf16[128,384]{1,0:T(8,128)(2,1)S(1)}, u32[]{:S(2)}, u32[]{:S(2)}) collective-permute-start(bf16[128,384]{1,0:T(8,128)(2,1)S(1)} %copy.13), channel_id=1, source_target_pairs={{0,4},{4,8},{8,12},{12,16},{16,20},{20,24},{24,28},{28,32},{32,36}... | collective-permute-start | bytes 294920 | tf_op jit(solution)/shard_map/while/body/eval_jaxpr/ppermute | solution.py:18
  21.1 10.0 %collective-permute-start.1 = (s32[128]{0:T(128)S(1)}, s32[128]{0:T(128)S(1)}, u32[]{:S(2)}, u32[]{:S(2)}) collective-permute-start(s32[128]{0:T(128)S(1)} %copy.14), channel_id=1, source_target_pairs={{0,4},{4,8},{8,12},{12,16},{16,20},{20,24},{24,28},{28,32},{32,36}... | collective-permute-start | bytes 1544 | tf_op jit(solution)/shard_map/while/body/eval_jaxpr/ppermute | solution.py:18
  23.9 11.2 %collective-permute-start.2 = (f32[128,384]{1,0:T(8,128)S(1)}, f32[128,384]{1,0:T(8,128)S(1)}, u32[]{:S(2)}, u32[]{:S(2)}) collective-permute-start(f32[128,384]{1,0:T(8,128)S(1)} %convolution_add_fusion.6), channel_id=1, source_target_pairs={{0,4},{4,8},{8,12},{12,16},{16,20},{20,24},{24,28},{28,32},{32,36}... | collective-permute-start | bytes 589832 | tf_op jit(solution)/shard_map/while/body/eval_jaxpr/ppermute | solution.py:18
  36.5 11.1 %collective-permute-start.2 = (f32[128,384]{1,0:T(8,128)S(1)}, f32[128,384]{1,0:T(8,128)S(1)}, u32[]{:S(2)}, u32[]{:S(2)}) collective-permute-start(f32[128,384]{1,0:T(8,128)S(1)} %convolution_add_fusion.6), channel_id=1, source_target_pairs={{0,4},{4,8},{8,12},{12,16},{16,20},{20,24},{24,28},{28,32},{32,36}... | collective-permute-start | bytes 589832 | tf_op jit(solution)/shard_map/while/body/eval_jaxpr/ppermute | solution.py:18
  49.1 10.7 %collective-permute-start.2 = (f32[128,384]{1,0:T(8,128)S(1)}, f32[128,384]{1,0:T(8,128)S(1)}, u32[]{:S(2)}, u32[]{:S(2)}) collective-permute-start(f32[128,384]{1,0:T(8,128)S(1)} %convolution_add_fusion.6), channel_id=1, source_target_pairs={{0,4},{4,8},{8,12},{12,16},{16,20},{20,24},{24,28},{28,32},{32,36}... | collective-permute-start | bytes 589832 | tf_op jit(solution)/shard_map/while/body/eval_jaxpr/ppermute | solution.py:18
  61.1 10.1 %collective-permute-start.2 = (f32[128,384]{1,0:T(8,128)S(1)}, f32[128,384]{1,0:T(8,128)S(1)}, u32[]{:S(2)}, u32[]{:S(2)}) collective-permute-start(f32[128,384]{1,0:T(8,128)S(1)} %convolution_add_fusion.6), channel_id=1, source_target_pairs={{0,4},{4,8},{8,12},{12,16},{16,20},{20,24},{24,28},{28,32},{32,36}... | collective-permute-start | bytes 589832 | tf_op jit(solution)/shard_map/while/body/eval_jaxpr/ppermute | solution.py:18
  72.7 9.6 %collective-permute-start.2 = (f32[128,384]{1,0:T(8,128)S(1)}, f32[128,384]{1,0:T(8,128)S(1)}, u32[]{:S(2)}, u32[]{:S(2)}) collective-permute-start(f32[128,384]{1,0:T(8,128)S(1)} %convolution_add_fusion.6), channel_id=1, source_target_pairs={{0,4},{4,8},{8,12},{12,16},{16,20},{20,24},{24,28},{28,32},{32,36}... | collective-permute-start | bytes 589832 | tf_op jit(solution)/shard_map/while/body/eval_jaxpr/ppermute | solution.py:18
  134.9 10.1 %collective-permute-start.2 = (f32[128,384]{1,0:T(8,128)S(1)}, f32[128,384]{1,0:T(8,128)S(1)}, u32[]{:S(2)}, u32[]{:S(2)}) collective-permute-start(f32[128,384]{1,0:T(8,128)S(1)} %convolution_add_fusion.6), channel_id=1, source_target_pairs={{0,4},{4,8},{8,12},{12,16},{16,20},{20,24},{24,28},{28,32},{32,36}... | collective-permute-start | bytes 589832 | tf_op jit(solution)/shard_map/while/body/eval_jaxpr/ppermute | solution.py:18
  146.4 11.3 %collective-permute-start.2 = (f32[128,384]{1,0:T(8,128)S(1)}, f32[128,384]{1,0:T(8,128)S(1)}, u32[]{:S(2)}, u32[]{:S(2)}) collective-permute-start(f32[128,384]{1,0:T(8,128)S(1)} %convolution_add_fusion.6), channel_id=1, source_target_pairs={{0,4},{4,8},{8,12},{12,16},{16,20},{20,24},{24,28},{28,32},{32,36}... | collective-permute-start | bytes 589832 | tf_op jit(solution)/shard_map/while/body/eval_jaxpr/ppermute | solution.py:18
  159.2 11.2 %collective-permute-start.2 = (f32[128,384]{1,0:T(8,128)S(1)}, f32[128,384]{1,0:T(8,128)S(1)}, u32[]{:S(2)}, u32[]{:S(2)}) collective-permute-start(f32[128,384]{1,0:T(8,128)S(1)} %convolution_add_fusion.6), channel_id=1, source_target_pairs={{0,4},{4,8},{8,12},{12,16},{16,20},{20,24},{24,28},{28,32},{32,36}... | collective-permute-start | bytes 589832 | tf_op jit(solution)/shard_map/while/body/eval_jaxpr/ppermute | solution.py:18
  171.7 11.0 %collective-permute-start.2 = (f32[128,384]{1,0:T(8,128)S(1)}, f32[128,384]{1,0:T(8,128)S(1)}, u32[]{:S(2)}, u32[]{:S(2)}) collective-permute-start(f32[128,384]{1,0:T(8,128)S(1)} %convolution_add_fusion.6), channel_id=1, source_target_pairs={{0,4},{4,8},{8,12},{12,16},{16,20},{20,24},{24,28},{28,32},{32,36}... | collective-permute-start | bytes 589832 | tf_op jit(solution)/shard_map/while/body/eval_jaxpr/ppermute | solution.py:18
  184.2 10.5 %collective-permute-start.2 = (f32[128,384]{1,0:T(8,128)S(1)}, f32[128,384]{1,0:T(8,128)S(1)}, u32[]{:S(2)}, u32[]{:S(2)}) collective-permute-start(f32[128,384]{1,0:T(8,128)S(1)} %convolution_add_fusion.6), channel_id=1, source_target_pairs={{0,4},{4,8},{8,12},{12,16},{16,20},{20,24},{24,28},{28,32},{32,36}... | collective-permute-start | bytes 589832 | tf_op jit(solution)/shard_map/while/body/eval_jaxpr/ppermute | solution.py:18
  196.1 10.0 %collective-permute-start.2 = (f32[128,384]{1,0:T(8,128)S(1)}, f32[128,384]{1,0:T(8,128)S(1)}, u32[]{:S(2)}, u32[]{:S(2)}) collective-permute-start(f32[128,384]{1,0:T(8,128)S(1)} %convolution_add_fusion.6), channel_id=1, source_target_pairs={{0,4},{4,8},{8,12},{12,16},{16,20},{20,24},{24,28},{28,32},{32,36}... | collective-permute-start | bytes 589832 | tf_op jit(solution)/shard_map/while/body/eval_jaxpr/ppermute | solution.py:18
  207.5 9.4 %collective-permute-start.2 = (f32[128,384]{1,0:T(8,128)S(1)}, f32[128,384]{1,0:T(8,128)S(1)}, u32[]{:S(2)}, u32[]{:S(2)}) collective-permute-start(f32[128,384]{1,0:T(8,128)S(1)} %convolution_add_fusion.6), channel_id=1, source_target_pairs={{0,4},{4,8},{8,12},{12,16},{16,20},{20,24},{24,28},{28,32},{32,36}... | collective-permute-start | bytes 589832 | tf_op jit(solution)/shard_map/while/body/eval_jaxpr/ppermute | solution.py:18
  268.2 9.1 %collective-permute-start = (bf16[128,384]{1,0:T(8,128)(2,1)S(1)}, bf16[128,384]{1,0:T(8,128)(2,1)S(1)}, u32[]{:S(2)}, u32[]{:S(2)}) collective-permute-start(bf16[128,384]{1,0:T(8,128)(2,1)S(1)} %copy.13), channel_id=1, source_target_pairs={{0,4},{4,8},{8,12},{12,16},{16,20},{20,24},{24,28},{28,32},{32,36}... | collective-permute-start | bytes 294920 | tf_op jit(solution)/shard_map/while/body/eval_jaxpr/ppermute | solution.py:18
  269.6 10.3 %collective-permute-start.2 = (f32[128,384]{1,0:T(8,128)S(1)}, f32[128,384]{1,0:T(8,128)S(1)}, u32[]{:S(2)}, u32[]{:S(2)}) collective-permute-start(f32[128,384]{1,0:T(8,128)S(1)} %convolution_add_fusion.6), channel_id=1, source_target_pairs={{0,4},{4,8},{8,12},{12,16},{16,20},{20,24},{24,28},{28,32},{32,36}... | collective-permute-start | bytes 589832 | tf_op jit(solution)/shard_map/while/body/eval_jaxpr/ppermute | solution.py:18
  281.4 11.6 %collective-permute-start.2 = (f32[128,384]{1,0:T(8,128)S(1)}, f32[128,384]{1,0:T(8,128)S(1)}, u32[]{:S(2)}, u32[]{:S(2)}) collective-permute-start(f32[128,384]{1,0:T(8,128)S(1)} %convolution_add_fusion.6), channel_id=1, source_target_pairs={{0,4},{4,8},{8,12},{12,16},{16,20},{20,24},{24,28},{28,32},{32,36}... | collective-permute-start | bytes 589832 | tf_op jit(solution)/shard_map/while/body/eval_jaxpr/ppermute | solution.py:18
  294.4 11.2 %collective-permute-start.2 = (f32[128,384]{1,0:T(8,128)S(1)}, f32[128,384]{1,0:T(8,128)S(1)}, u32[]{:S(2)}, u32[]{:S(2)}) collective-permute-start(f32[128,384]{1,0:T(8,128)S(1)} %convolution_add_fusion.6), channel_id=1, source_target_pairs={{0,4},{4,8},{8,12},{12,16},{16,20},{20,24},{24,28},{28,32},{32,36}... | collective-permute-start | bytes 589832 | tf_op jit(solution)/shard_map/while/body/eval_jaxpr/ppermute | solution.py:18
  307.0 11.0 %collective-permute-start.2 = (f32[128,384]{1,0:T(8,128)S(1)}, f32[128,384]{1,0:T(8,128)S(1)}, u32[]{:S(2)}, u32[]{:S(2)}) collective-permute-start(f32[128,384]{1,0:T(8,128)S(1)} %convolution_add_fusion.6), channel_id=1, source_target_pairs={{0,4},{4,8},{8,12},{12,16},{16,20},{20,24},{24,28},{28,32},{32,36}... | collective-permute-start | bytes 589832 | tf_op jit(solution)/shard_map/while/body/eval_jaxpr/ppermute | solution.py:18
  319.4 10.5 %collective-permute-start.2 = (f32[128,384]{1,0:T(8,128)S(1)}, f32[128,384]{1,0:T(8,128)S(1)}, u32[]{:S(2)}, u32[]{:S(2)}) collective-permute-start(f32[128,384]{1,0:T(8,128)S(1)} %convolution_add_fusion.6), channel_id=1, source_target_pairs={{0,4},{4,8},{8,12},{12,16},{16,20},{20,24},{24,28},{28,32},{32,36}... | collective-permute-start | bytes 589832 | tf_op jit(solution)/shard_map/while/body/eval_jaxpr/ppermute | solution.py:18
  331.3 10.0 %collective-permute-start.2 = (f32[128,384]{1,0:T(8,128)S(1)}, f32[128,384]{1,0:T(8,128)S(1)}, u32[]{:S(2)}, u32[]{:S(2)}) collective-permute-start(f32[128,384]{1,0:T(8,128)S(1)} %convolution_add_fusion.6), channel_id=1, source_target_pairs={{0,4},{4,8},{8,12},{12,16},{16,20},{20,24},{24,28},{28,32},{32,36}... | collective-permute-start | bytes 589832 | tf_op jit(solution)/shard_map/while/body/eval_jaxpr/ppermute | solution.py:18
  342.8 9.4 %collective-permute-start.2 = (f32[128,384]{1,0:T(8,128)S(1)}, f32[128,384]{1,0:T(8,128)S(1)}, u32[]{:S(2)}, u32[]{:S(2)}) collective-permute-start(f32[128,384]{1,0:T(8,128)S(1)} %convolution_add_fusion.6), channel_id=1, source_target_pairs={{0,4},{4,8},{8,12},{12,16},{16,20},{20,24},{24,28},{28,32},{32,36}... | collective-permute-start | bytes 589832 | tf_op jit(solution)/shard_map/while/body/eval_jaxpr/ppermute | solution.py:18
  403.5 9.1 %collective-permute-start = (bf16[128,384]{1,0:T(8,128)(2,1)S(1)}, bf16[128,384]{1,0:T(8,128)(2,1)S(1)}, u32[]{:S(2)}, u32[]{:S(2)}) collective-permute-start(bf16[128,384]{1,0:T(8,128)(2,1)S(1)} %copy.13), channel_id=1, source_target_pairs={{0,4},{4,8},{8,12},{12,16},{16,20},{20,24},{24,28},{28,32},{32,36}... | collective-permute-start | bytes 294920 | tf_op jit(solution)/shard_map/while/body/eval_jaxpr/ppermute | solution.py:18
  404.9 10.3 %collective-permute-start.2 = (f32[128,384]{1,0:T(8,128)S(1)}, f32[128,384]{1,0:T(8,128)S(1)}, u32[]{:S(2)}, u32[]{:S(2)}) collective-permute-start(f32[128,384]{1,0:T(8,128)S(1)} %convolution_add_fusion.6), channel_id=1, source_target_pairs={{0,4},{4,8},{8,12},{12,16},{16,20},{20,24},{24,28},{28,32},{32,36}... | collective-permute-start | bytes 589832 | tf_op jit(solution)/shard_map/while/body/eval_jaxpr/ppermute | solution.py:18
  415.2 9.1 %collective-permute-start = (bf16[128,384]{1,0:T(8,128)(2,1)S(1)}, bf16[128,384]{1,0:T(8,128)(2,1)S(1)}, u32[]{:S(2)}, u32[]{:S(2)}) collective-permute-start(bf16[128,384]{1,0:T(8,128)(2,1)S(1)} %copy.13), channel_id=1, source_target_pairs={{0,4},{4,8},{8,12},{12,16},{16,20},{20,24},{24,28},{28,32},{32,36}... | collective-permute-start | bytes 294920 | tf_op jit(solution)/shard_map/while/body/eval_jaxpr/ppermute | solution.py:18
  416.6 11.6 %collective-permute-start.2 = (f32[128,384]{1,0:T(8,128)S(1)}, f32[128,384]{1,0:T(8,128)S(1)}, u32[]{:S(2)}, u32[]{:S(2)}) collective-permute-start(f32[128,384]{1,0:T(8,128)S(1)} %convolution_add_fusion.6), channel_id=1, source_target_pairs={{0,4},{4,8},{8,12},{12,16},{16,20},{20,24},{24,28},{28,32},{32,36}... | collective-permute-start | bytes 589832 | tf_op jit(solution)/shard_map/while/body/eval_jaxpr/ppermute | solution.py:18
  429.7 11.2 %collective-permute-start.2 = (f32[128,384]{1,0:T(8,128)S(1)}, f32[128,384]{1,0:T(8,128)S(1)}, u32[]{:S(2)}, u32[]{:S(2)}) collective-permute-start(f32[128,384]{1,0:T(8,128)S(1)} %convolution_add_fusion.6), channel_id=1, source_target_pairs={{0,4},{4,8},{8,12},{12,16},{16,20},{20,24},{24,28},{28,32},{32,36}... | collective-permute-start | bytes 589832 | tf_op jit(solution)/shard_map/while/body/eval_jaxpr/ppermute | solution.py:18
  442.2 11.0 %collective-permute-start.2 = (f32[128,384]{1,0:T(8,128)S(1)}, f32[128,384]{1,0:T(8,128)S(1)}, u32[]{:S(2)}, u32[]{:S(2)}) collective-permute-start(f32[128,384]{1,0:T(8,128)S(1)} %convolution_add_fusion.6), channel_id=1, source_target_pairs={{0,4},{4,8},{8,12},{12,16},{16,20},{20,24},{24,28},{28,32},{32,36}... | collective-permute-start | bytes 589832 | tf_op jit(solution)/shard_map/while/body/eval_jaxpr/ppermute | solution.py:18
  454.6 10.5 %collective-permute-start.2 = (f32[128,384]{1,0:T(8,128)S(1)}, f32[128,384]{1,0:T(8,128)S(1)}, u32[]{:S(2)}, u32[]{:S(2)}) collective-permute-start(f32[128,384]{1,0:T(8,128)S(1)} %convolution_add_fusion.6), channel_id=1, source_target_pairs={{0,4},{4,8},{8,12},{12,16},{16,20},{20,24},{24,28},{28,32},{32,36}... | collective-permute-start | bytes 589832 | tf_op jit(solution)/shard_map/while/body/eval_jaxpr/ppermute | solution.py:18
  466.6 10.0 %collective-permute-start.2 = (f32[128,384]{1,0:T(8,128)S(1)}, f32[128,384]{1,0:T(8,128)S(1)}, u32[]{:S(2)}, u32[]{:S(2)}) collective-permute-start(f32[128,384]{1,0:T(8,128)S(1)} %convolution_add_fusion.6), channel_id=1, source_target_pairs={{0,4},{4,8},{8,12},{12,16},{16,20},{20,24},{24,28},{28,32},{32,36}... | collective-permute-start | bytes 589832 | tf_op jit(solution)/shard_map/while/body/eval_jaxpr/ppermute | solution.py:18
  478.0 9.4 %collective-permute-start.2 = (f32[128,384]{1,0:T(8,128)S(1)}, f32[128,384]{1,0:T(8,128)S(1)}, u32[]{:S(2)}, u32[]{:S(2)}) collective-permute-start(f32[128,384]{1,0:T(8,128)S(1)} %convolution_add_fusion.6), channel_id=1, source_target_pairs={{0,4},{4,8},{8,12},{12,16},{16,20},{20,24},{24,28},{28,32},{32,36}... | collective-permute-start | bytes 589832 | tf_op jit(solution)/shard_map/while/body/eval_jaxpr/ppermute | solution.py:18
  538.7 9.1 %collective-permute-start = (bf16[128,384]{1,0:T(8,128)(2,1)S(1)}, bf16[128,384]{1,0:T(8,128)(2,1)S(1)}, u32[]{:S(2)}, u32[]{:S(2)}) collective-permute-start(bf16[128,384]{1,0:T(8,128)(2,1)S(1)} %copy.13), channel_id=1, source_target_pairs={{0,4},{4,8},{8,12},{12,16},{16,20},{20,24},{24,28},{28,32},{32,36}... | collective-permute-start | bytes 294920 | tf_op jit(solution)/shard_map/while/body/eval_jaxpr/ppermute | solution.py:18
  540.1 10.3 %collective-permute-start.2 = (f32[128,384]{1,0:T(8,128)S(1)}, f32[128,384]{1,0:T(8,128)S(1)}, u32[]{:S(2)}, u32[]{:S(2)}) collective-permute-start(f32[128,384]{1,0:T(8,128)S(1)} %convolution_add_fusion.6), channel_id=1, source_target_pairs={{0,4},{4,8},{8,12},{12,16},{16,20},{20,24},{24,28},{28,32},{32,36}... | collective-permute-start | bytes 589832 | tf_op jit(solution)/shard_map/while/body/eval_jaxpr/ppermute | solution.py:18
  550.5 9.1 %collective-permute-start = (bf16[128,384]{1,0:T(8,128)(2,1)S(1)}, bf16[128,384]{1,0:T(8,128)(2,1)S(1)}, u32[]{:S(2)}, u32[]{:S(2)}) collective-permute-start(bf16[128,384]{1,0:T(8,128)(2,1)S(1)} %copy.13), channel_id=1, source_target_pairs={{0,4},{4,8},{8,12},{12,16},{16,20},{20,24},{24,28},{28,32},{32,36}... | collective-permute-start | bytes 294920 | tf_op jit(solution)/shard_map/while/body/eval_jaxpr/ppermute | solution.py:18
  551.9 11.6 %collective-permute-start.2 = (f32[128,384]{1,0:T(8,128)S(1)}, f32[128,384]{1,0:T(8,128)S(1)}, u32[]{:S(2)}, u32[]{:S(2)}) collective-permute-start(f32[128,384]{1,0:T(8,128)S(1)} %convolution_add_fusion.6), channel_id=1, source_target_pairs={{0,4},{4,8},{8,12},{12,16},{16,20},{20,24},{24,28},{28,32},{32,36}... | collective-permute-start | bytes 589832 | tf_op jit(solution)/shard_map/while/body/eval_jaxpr/ppermute | solution.py:18
  564.9 11.2 %collective-permute-start.2 = (f32[128,384]{1,0:T(8,128)S(1)}, f32[128,384]{1,0:T(8,128)S(1)}, u32[]{:S(2)}, u32[]{:S(2)}) collective-permute-start(f32[128,384]{1,0:T(8,128)S(1)} %convolution_add_fusion.6), channel_id=1, source_target_pairs={{0,4},{4,8},{8,12},{12,16},{16,20},{20,24},{24,28},{28,32},{32,36}... | collective-permute-start | bytes 589832 | tf_op jit(solution)/shard_map/while/body/eval_jaxpr/ppermute | solution.py:18
  577.5 11.0 %collective-permute-start.2 = (f32[128,384]{1,0:T(8,128)S(1)}, f32[128,384]{1,0:T(8,128)S(1)}, u32[]{:S(2)}, u32[]{:S(2)}) collective-permute-start(f32[128,384]{1,0:T(8,128)S(1)} %convolution_add_fusion.6), channel_id=1, source_target_pairs={{0,4},{4,8},{8,12},{12,16},{16,20},{20,24},{24,28},{28,32},{32,36}... | collective-permute-start | bytes 589832 | tf_op jit(solution)/shard_map/while/body/eval_jaxpr/ppermute | solution.py:18
  589.9 10.5 %collective-permute-start.2 = (f32[128,384]{1,0:T(8,128)S(1)}, f32[128,384]{1,0:T(8,128)S(1)}, u32[]{:S(2)}, u32[]{:S(2)}) collective-permute-start(f32[128,384]{1,0:T(8,128)S(1)} %convolution_add_fusion.6), channel_id=1, source_target_pairs={{0,4},{4,8},{8,12},{12,16},{16,20},{20,24},{24,28},{28,32},{32,36}... | collective-permute-start | bytes 589832 | tf_op jit(solution)/shard_map/while/body/eval_jaxpr/ppermute | solution.py:18
  601.8 10.0 %collective-permute-start.2 = (f32[128,384]{1,0:T(8,128)S(1)}, f32[128,384]{1,0:T(8,128)S(1)}, u32[]{:S(2)}, u32[]{:S(2)}) collective-permute-start(f32[128,384]{1,0:T(8,128)S(1)} %convolution_add_fusion.6), channel_id=1, source_target_pairs={{0,4},{4,8},{8,12},{12,16},{16,20},{20,24},{24,28},{28,32},{32,36}... | collective-permute-start | bytes 589832 | tf_op jit(solution)/shard_map/while/body/eval_jaxpr/ppermute | solution.py:18
  613.2 9.4 %collective-permute-start.2 = (f32[128,384]{1,0:T(8,128)S(1)}, f32[128,384]{1,0:T(8,128)S(1)}, u32[]{:S(2)}, u32[]{:S(2)}) collective-permute-start(f32[128,384]{1,0:T(8,128)S(1)} %convolution_add_fusion.6), channel_id=1, source_target_pairs={{0,4},{4,8},{8,12},{12,16},{16,20},{20,24},{24,28},{28,32},{32,36}... | collective-permute-start | bytes 589832 | tf_op jit(solution)/shard_map/while/body/eval_jaxpr/ppermute | solution.py:18
  674.0 9.1 %collective-permute-start = (bf16[128,384]{1,0:T(8,128)(2,1)S(1)}, bf16[128,384]{1,0:T(8,128)(2,1)S(1)}, u32[]{:S(2)}, u32[]{:S(2)}) collective-permute-start(bf16[128,384]{1,0:T(8,128)(2,1)S(1)} %copy.13), channel_id=1, source_target_pairs={{0,4},{4,8},{8,12},{12,16},{16,20},{20,24},{24,28},{28,32},{32,36}... | collective-permute-start | bytes 294920 | tf_op jit(solution)/shard_map/while/body/eval_jaxpr/ppermute | solution.py:18
  675.4 10.3 %collective-permute-start.2 = (f32[128,384]{1,0:T(8,128)S(1)}, f32[128,384]{1,0:T(8,128)S(1)}, u32[]{:S(2)}, u32[]{:S(2)}) collective-permute-start(f32[128,384]{1,0:T(8,128)S(1)} %convolution_add_fusion.6), channel_id=1, source_target_pairs={{0,4},{4,8},{8,12},{12,16},{16,20},{20,24},{24,28},{28,32},{32,36}... | collective-permute-start | bytes 589832 | tf_op jit(solution)/shard_map/while/body/eval_jaxpr/ppermute | solution.py:18
  687.1 11.6 %collective-permute-start.2 = (f32[128,384]{1,0:T(8,128)S(1)}, f32[128,384]{1,0:T(8,128)S(1)}, u32[]{:S(2)}, u32[]{:S(2)}) collective-permute-start(f32[128,384]{1,0:T(8,128)S(1)} %convolution_add_fusion.6), channel_id=1, source_target_pairs={{0,4},{4,8},{8,12},{12,16},{16,20},{20,24},{24,28},{28,32},{32,36}... | collective-permute-start | bytes 589832 | tf_op jit(solution)/shard_map/while/body/eval_jaxpr/ppermute | solution.py:18
  700.1 11.2 %collective-permute-start.2 = (f32[128,384]{1,0:T(8,128)S(1)}, f32[128,384]{1,0:T(8,128)S(1)}, u32[]{:S(2)}, u32[]{:S(2)}) collective-permute-start(f32[128,384]{1,0:T(8,128)S(1)} %convolution_add_fusion.6), channel_id=1, source_target_pairs={{0,4},{4,8},{8,12},{12,16},{16,20},{20,24},{24,28},{28,32},{32,36}... | collective-permute-start | bytes 589832 | tf_op jit(solution)/shard_map/while/body/eval_jaxpr/ppermute | solution.py:18
  712.7 11.0 %collective-permute-start.2 = (f32[128,384]{1,0:T(8,128)S(1)}, f32[128,384]{1,0:T(8,128)S(1)}, u32[]{:S(2)}, u32[]{:S(2)}) collective-permute-start(f32[128,384]{1,0:T(8,128)S(1)} %convolution_add_fusion.6), channel_id=1, source_target_pairs={{0,4},{4,8},{8,12},{12,16},{16,20},{20,24},{24,28},{28,32},{32,36}... | collective-permute-start | bytes 589832 | tf_op jit(solution)/shard_map/while/body/eval_jaxpr/ppermute | solution.py:18
  725.1 10.5 %collective-permute-start.2 = (f32[128,384]{1,0:T(8,128)S(1)}, f32[128,384]{1,0:T(8,128)S(1)}, u32[]{:S(2)}, u32[]{:S(2)}) collective-permute-start(f32[128,384]{1,0:T(8,128)S(1)} %convolution_add_fusion.6), channel_id=1, source_target_pairs={{0,4},{4,8},{8,12},{12,16},{16,20},{20,24},{24,28},{28,32},{32,36}... | collective-permute-start | bytes 589832 | tf_op jit(solution)/shard_map/while/body/eval_jaxpr/ppermute | solution.py:18
  737.4 10.4 %collective-permute-start.3 = (f32[128,384]{1,0:T(8,128)S(1)}, f32[128,384]{1,0:T(8,128)S(1)}, u32[]{:S(2)}, u32[]{:S(2)}) collective-permute-start(f32[128,384]{1,0:T(8,128)S(1)} %convolution_add_fusion.3), channel_id=1, source_target_pairs={{0,4},{4,8},{8,12},{12,16},{16,20},{20,24},{24,28},{28,32},{32,36}... | collective-permute-start | bytes 589832 | tf_op jit(solution)/shard_map/ppermute | solution.py:18
  (146 other events, 1167.1 us)
Sparse Core Ops, SparseCore 0:
  737.3 92.2 reduce-scatter.1
where the time goes:
time: 838 us; the launch traced here: 837 us
  waiting for transfers between devices  684 us (82%)
  matrix products  100 us (12%)
  starting transfers between devices  18.1 us (2%)
  between operations  15.4 us (2%)
  blocking collectives  10.7 us (1%)
    ppermute x190, waiting for transfers between devices, passed_along(): return lax.ppermute(value, axis, pairs)  602 us
    reduce_scatter x1, waiting for transfers between devices, per_device(): lax.psum_scatter(portion, 'narrow', scatter_dimension=0, tiled=True)  81.8 us
    dot_general x64, matrix products, weigh(): lax.dot_general(low_rows, high_rows, (((1,), (1,)), ((), ())), preferred_...  60.8 us
    dot_general x64, matrix products, absorb(): lax.dot_general(weights, low_rows, (((0,), (0,)), ((), ())), preferred_el...  25 us
    ppermute x190, starting transfers between devices, passed_along(): return lax.ppermute(value, axis, pairs)  18.1 us
  transfers between devices with their start and end apart: 191, of which 128 were waited for; matrix products, arithmetic and copies ran while one was open for 12% of the time, Pallas kernels for 0%

commit v1 on v0

v1 whole, which is shorter than its diff:
```python
import functools

import jax
import jax.numpy as jnp
from jax import lax
from jax.experimental import pallas as pl
from jax.experimental.pallas import tpu as pltpu
from jax.sharding import PartitionSpec as P

MESH = pl.DeviceIdType.MESH
F32, BF16 = jnp.float32, jnp.bfloat16
X, Y, Z = 4, 4, 8
ROWS, WIDTH = 128, 384
HALF = WIDTH // 2

NEAR = [(0, 0), (1, 0), (3, 0), (0, 1), (0, 3), (2, 0), (0, 2)]
FAR = [(1, 1), (3, 3), (1, 3), (3, 1), (2, 1), (1, 2), (2, 3), (3, 2), (2, 2)]
LOW_AT = {slot: i for i, slot in enumerate(NEAR + FAR)}
HIGH_AT = {(dz, dc): 2 * i + dc for i, dz in enumerate((0, 1, 7, 2, 6, 3, 5, 4)) for dc in (0, 1)}
GROUP = 8
BLOCK = GROUP * ROWS


def dot(a, b, over):
    return lax.dot_general(a, b, (over, ((), ())), preferred_element_type=F32)


def kernel(
    low_in, high_in, partner_in, factors,
    low_out, high_out,
    low, high, part, prow, weights, gl, gh,
    got_a, got_b, sum_a, sum_b, last_a, last_b,
    got_core, got_three, got_four, got_two, got_one,
    send_sems, recv_sems,
):
    blk, narrow = lax.axis_index("blk"), lax.axis_index("narrow")
    x, z, y, core = blk // 16, (blk // 2) % 8, (narrow // 2) * 2 + blk % 2, narrow % 2

    def device(dx=0, dy=0, dz=0, dc=0):
        px, py, pz, pc = (x + dx) % X, (y + dy) % Y, (z + dz) % Z, (core + dc) % 2
        return ((px * Z + pz) * 2 + py % 2, (py // 2) * 2 + pc)

    copies = []

    def send(src, dst, **to):
        k = len(copies)
        copy = pltpu.make_async_remote_copy(
            src, dst, send_sems.at[k], recv_sems.at[k], device_id=device(**to), device_id_type=MESH
        )
        copy.start()
        copies.append(copy)
        return copy

    def low_rows(slot, first=0, count=ROWS):
        return pl.ds(LOW_AT[slot] * ROWS + first, count)

    def low_cols(slot):
        return pl.ds(LOW_AT[slot] * ROWS, ROWS)

    def high_rows(dz, dc, first=0, count=ROWS):
        return pl.ds(HIGH_AT[dz, dc] * ROWS + first, count)

    a_rows, b_rows = pl.ds(0, HALF), pl.ds(HALF, HALF)

    peers = [dict(dx=e) for e in (1, 2, 3)] + [dict(dy=e) for e in (1, 2, 3)]
    peers += [dict(dz=e) for e in (1, 2, 6, 7)] + [dict(dc=1)]
    barrier = pltpu.get_barrier_semaphore()
    for peer in peers:
        pl.semaphore_signal(barrier, inc=1, device_id=device(**peer), device_id_type=MESH)
    low[low_rows((0, 0)), :] = low_in[...]
    high[high_rows(0, 0), :] = high_in[...]
    part[0, 0] = jnp.broadcast_to(partner_in[...], (8, ROWS))
    pl.semaphore_wait(barrier, len(peers))

    low_x, low_y, low_a, low_b, part_x, part_y, high_same, high_other = {}, {}, {}, {}, {}, {}, {}, {}
    for e in (2, 6):
        high_same[8 - e] = send(high_in, high.at[high_rows(8 - e, 0)], dz=e)
    for e in (1, 3):
        part_x[4 - e] = send(part.at[0, 0], part.at[0, 4 - e], dx=e)
        low_x[4 - e] = send(low_in, low.at[low_rows((4 - e, 0))], dx=e)
        low_y[4 - e] = send(low_in, low.at[low_rows((0, 4 - e))], dy=e)
    high_other[0] = send(high_in, high.at[high_rows(0, 1)], dc=1)
    for e in (1, 7):
        high_same[8 - e] = send(high_in, high.at[high_rows(8 - e, 0)], dz=e)
    part_x[2] = send(part.at[0, 0], part.at[0, 2], dx=2)
    low_x[2] = send(low_in, low.at[low_rows((2, 0))], dx=2)
    low_y[2] = send(low_in, low.at[low_rows((0, 2))], dy=2)

    def to_other_core(dz):
        rows = high_rows(dz, 0)
        high_other[dz] = send(high.at[rows], high.at[high_rows(dz, 1)], dc=1)

    def pass_low(d):
        low_x[d].wait_recv()
        for e in (1, 3, 2):
            src = low.at[low_rows((d, 0), 0, 64)]
            low_a[d, 4 - e] = send(src, low.at[low_rows((d, 4 - e), 0, 64)], dy=e)
        low_y[d].wait_recv()
        for e in (1, 3, 2):
            src = low.at[low_rows((0, d), 64, 64)]
            low_b[4 - e, d] = send(src, low.at[low_rows((4 - e, d), 64, 64)], dx=e)

    pass_low(1)
    pass_low(3)
    for e in (1, 3, 2):
        part_x[e].wait_recv()
    for e in (1, 3, 2):
        part_y[4 - e] = send(part.at[0], part.at[4 - e], dy=e)
    high_same[6].wait_recv()
    high_same[5] = send(high.at[high_rows(6, 0)], high.at[high_rows(5, 0)], dz=1)
    four_a = send(high.at[high_rows(6, 0, 0, 64)], high.at[high_rows(4, 0, 0, 64)], dz=2)
    high_same[2].wait_recv()
    high_same[3] = send(high.at[high_rows(2, 0)], high.at[high_rows(3, 0)], dz=7)
    four_b = send(high.at[high_rows(2, 0, 64, 64)], high.at[high_rows(4, 0, 64, 64)], dz=6)
    pass_low(2)
    to_other_core(2)
    to_other_core(6)
    for dz in (1, 7):
        high_same[dz].wait_recv()
        to_other_core(dz)

    scale, bias = factors[0], factors[1]
    gain, shift, half = 0.5 * scale, 0.5 * bias, 0.5 * scale
    started = set()

    def add_to(ref, index, key, value):
        if key in started:
            ref[index] += value
        else:
            ref[index] = value
            started.add(key)

    def block(lg, hg):
        cols, rows = pl.ds(lg * BLOCK, BLOCK), pl.ds(hg * BLOCK, BLOCK)
        low_block, high_block = low[cols, :], high[rows, :]
        logits = dot(high_block, low_block, ((1,), (1,)))
        wanted = prow[:, cols]
        for i in range(GROUP):
            dz, dc = next(k for k, v in HIGH_AT.items() if v == hg * GROUP + i)
            b, n = device(dz=dz, dc=dc)
            first = (b * 4 + n) * ROWS
            here = slice(i * ROWS, (i + 1) * ROWS)
            ids = lax.broadcasted_iota(jnp.int32, (ROWS, BLOCK), 0)
            match = ids == wanted - first
            value = jnp.tanh(logits[here] * gain + shift) * half + jnp.where(match, -half, half)
            weights[here, :] = value.astype(BF16)
        w = weights[...]
        add_to(gh, (rows, slice(None)), ("h", hg), dot(w, low_block, ((1,), (0,))))
        add_to(gl, (slice(None), cols), ("l", lg), dot(high_block, w, ((0,), (0,))))

    def take_part(slots):
        for dx, dy in slots:
            prow[:, low_cols((dx, dy))] = part[dy, dx, 0:1, :]

    high_other[0].wait_recv()
    for dz in (1, 7, 2):
        high_other[dz].wait_recv()
    low_a[1, 1].wait_recv()
    low_b[1, 1].wait_recv()
    for e in (1, 2, 3):
        part_y[e].wait_recv()
    take_part(NEAR + FAR)
    block(0, 0)
    for dz in (3, 5):
        high_same[dz].wait_recv()
        to_other_core(dz)
    four_a.wait_recv()
    four_b.wait_recv()
    to_other_core(4)
    for slot in FAR[1:]:
        low_a[slot].wait_recv()
        low_b[slot].wait_recv()
    for dz in (6, 3, 5, 4):
        high_other[dz].wait_recv()
    block(1, 1)
    block(0, 1)

    from_core = {}

    def core_sum_send(dz):
        from_core[dz] = send(gh.at[high_rows(dz, 1)], got_core.at[dz], dc=1)

    def core_sum_take(dz):
        from_core[dz].wait_recv()
        gh[high_rows(dz, 0), :] += got_core[dz]

    for dz in (4, 3, 5, 6):
        core_sum_send(dz)
    block(1, 0)
    for dz in (2, 1, 7, 0):
        core_sum_send(dz)

    a_far, b_far, a_near, b_near = {}, {}, {}, {}
    for e in (1, 3, 2):
        for d in (2, 1, 3, 0):
            a_far[4 - e, d] = send(gl.at[a_rows, low_cols((d, e))], got_a.at[4 - e, d], dy=e)
            b_far[4 - e, d] = send(gl.at[b_rows, low_cols((e, d))], got_b.at[4 - e, d], dx=e)

    for dz in (4, 3, 5, 6, 2):
        core_sum_take(dz)
    four_a = send(gh.at[high_rows(4, 0, 0, 64)], got_four.at[0], dz=2)
    four_b = send(gh.at[high_rows(4, 0, 64, 64)], got_four.at[1], dz=6)
    three_a = send(gh.at[high_rows(3, 0)], got_three.at[0], dz=1)
    three_b = send(gh.at[high_rows(5, 0)], got_three.at[1], dz=7)
    for dz in (1, 7):
        core_sum_take(dz)
    one_a = send(gh.at[high_rows(1, 0)], got_one.at[0], dz=1)
    one_b = send(gh.at[high_rows(7, 0)], got_one.at[1], dz=7)

    three_a.wait_recv()
    four_a.wait_recv()
    gh[high_rows(2, 0), :] += got_three[0]
    gh[high_rows(2, 0, 0, 64), :] += got_four[0]
    two_a = send(gh.at[high_rows(2, 0)], got_two.at[0], dz=2)
    three_b.wait_recv()
    four_b.wait_recv()
    gh[high_rows(6, 0), :] += got_three[1]
    gh[high_rows(6, 0, 64, 64), :] += got_four[1]
    two_b = send(gh.at[high_rows(6, 0)], got_two.at[1], dz=6)

    for d in (2, 1, 3):
        for e in (1, 3, 2):
            a_far[e, d].wait_recv()
            b_far[e, d].wait_recv()
        sum_a[d] = gl[a_rows, low_cols((d, 0))] + got_a[1, d] + got_a[2, d] + got_a[3, d]
        a_near[d] = send(sum_a.at[d], last_a.at[d], dx=d)
        sum_b[d] = gl[b_rows, low_cols((0, d))] + got_b[1, d] + got_b[2, d] + got_b[3, d]
        b_near[d] = send(sum_b.at[d], last_b.at[d], dy=d)

    core_sum_take(0)
    for copy in (one_a, one_b, two_a, two_b):
        copy.wait_recv()
    high_out[...] = gh[high_rows(0, 0), :] + got_one[0] + got_one[1] + got_two[0] + got_two[1]
    for e in (1, 3, 2):
        a_far[e, 0].wait_recv()
        b_far[e, 0].wait_recv()
    for d in (1, 3, 2):
        a_near[d].wait_recv()
        b_near[d].wait_recv()
    total_a = gl[a_rows, low_cols((0, 0))] + got_a[1, 0] + got_a[2, 0] + got_a[3, 0]
    total_a += last_a[1] + last_a[2] + last_a[3]
    total_b = gl[b_rows, low_cols((0, 0))] + got_b[1, 0] + got_b[2, 0] + got_b[3, 0]
    total_b += last_b[1] + last_b[2] + last_b[3]
    low_out[...] = jnp.concatenate([total_a, total_b], axis=0).T
    for copy in copies:
        copy.wait_send()


def per_device(embed_low, embed_high, partner, log_scale, bias):
    factors = jnp.stack([jnp.exp(log_scale), bias])
    vmem, smem = pl.BlockSpec(memory_space=pltpu.VMEM), pl.BlockSpec(memory_space=pltpu.SMEM)
    group = 2 * BLOCK
    grad = jax.ShapeDtypeStruct((ROWS, WIDTH), F32)
    return pl.pallas_call(
        kernel,
        out_shape=(grad, grad),
        in_specs=[vmem, vmem, vmem, smem],
        out_specs=(vmem, vmem),
        scratch_shapes=[
            pltpu.VMEM((group, WIDTH), BF16),
            pltpu.VMEM((group, WIDTH), BF16),
            pltpu.VMEM((4, 4, 8, ROWS), jnp.int32),
            pltpu.VMEM((1, group), jnp.int32),
            pltpu.VMEM((BLOCK, BLOCK), BF16),
            pltpu.VMEM((WIDTH, group), F32),
            pltpu.VMEM((group, WIDTH), F32),
            pltpu.VMEM((4, 4, HALF, ROWS), F32),
            pltpu.VMEM((4, 4, HALF, ROWS), F32),
            pltpu.VMEM((4, HALF, ROWS), F32),
            pltpu.VMEM((4, HALF, ROWS), F32),
            pltpu.VMEM((4, HALF, ROWS), F32),
            pltpu.VMEM((4, HALF, ROWS), F32),
            pltpu.VMEM((8, ROWS, WIDTH), F32),
            pltpu.VMEM((2, ROWS, WIDTH), F32),
            pltpu.VMEM((2, ROWS // 2, WIDTH), F32),
            pltpu.VMEM((2, ROWS, WIDTH), F32),
            pltpu.VMEM((2, ROWS, WIDTH), F32),
            pltpu.SemaphoreType.DMA((96,)),
            pltpu.SemaphoreType.DMA((96,)),
        ],
        compiler_params=pltpu.CompilerParams(
            collective_id=0, has_side_effects=True, vmem_limit_bytes=56 * 2**20
        ),
    )(embed_low, embed_high, partner.reshape(1, ROWS), factors)


def solution(mesh):
    in_specs = (
        P(("blk", "narrow"), None),
        P(("blk", "narrow"), None),
        P(("blk", "narrow")),
        P(),
        P(),
    )
    out_specs = (P(("blk", "narrow"), None), P(("blk", "narrow"), None))
    return jax.shard_map(
        per_device, mesh=mesh, in_specs=in_specs, out_specs=out_specs, check_vma=False
    )
```

time: 838 us -> 68.9 us (0.08)
  waiting for transfers between devices: 684 us -> 0 us
  matrix products: 100 us -> 0 us
  Pallas kernels: 0 us -> 63.8 us
  starting transfers between devices: 18.1 us -> 0 us
  between operations: 15.4 us -> 1.98 us
  blocking collectives: 10.7 us -> 0 us
    ppermute x190 -> x0, waiting for transfers between devices: 602 us -> none  [passed_along(): return lax.ppermute(value, axis, pairs)]
    dot_general x192 -> x0, matrix products: 100 us -> none  [the longest x64 60.8 us: weigh(): lax.dot_general(low_rows, high_rows, (((1,), (1,)), ((), ())), preferred_...]
    reduce_scatter x1 -> x0, waiting for transfers between devices: 81.8 us -> none  [per_device(): lax.psum_scatter(portion, 'narrow', scatter_dimension=0, tiled=True)]
    pallas_call x0 -> x1, Pallas kernels: none -> 63.8 us  [per_device(): pl.pallas_call(kernel, out_shape=(grad, grad), in_specs=[vmem, vmem, vmem...]
    ppermute x190 -> x0, starting transfers between devices: 18.1 us -> none  [passed_along(): return lax.ppermute(value, axis, pairs)]
    all_gather x1 -> x0, blocking collectives: 10.7 us -> none  [per_device(): high_group = lax.all_gather(embed_high, 'narrow', axis=0, tiled=True)]
  transfers between devices with their start and end apart: 191 -> 0, of which waited for: 128 -> 0; matrix products, arithmetic and copies ran while one was open for 12% -> 0% of each run, Pallas kernels for 0% -> 0%
where the time goes in v1:
time: 68.9 us; the launch traced here: 68.7 us
  Pallas kernels  63.8 us (93%)
  local copies, waits for them, and re-layouts  2.34 us (3%)
  between operations  1.98 us (3%)
    pallas_call x1, Pallas kernels, per_device(): pl.pallas_call(kernel, out_shape=(grad, grad), in_specs=[vmem, vmem, vmem...  63.8 us
    unnamed x4, local copies, waits for them, and re-layouts  2.34 us

profile of v1, /device:TPU:1, one launch (start us, length us, event | category | flops | bytes accessed | tf_op | source)
XLA Modules:
  0.0 68.7 jit_solution(2703848435981555407)
XLA Ops:
  2.0 0.7 pad_maximum_fusion.factors
  2.6 63.8 %shard_map.68 = (f32[128,384]{1,0:T(8,128)}, f32[128,384]{1,0:T(8,128)}) custom-call(bf16[128,384]{1,0:T(8,128)(2,1)} %low_in.1, bf16[128,384]{1,0:T(8,128)(2,1)} %high_in.1, s32[1,128]{1,0:T(1,128)} %bitcast.4, f32[2]{0:T(128)} %pad_maximum_fusion.factors), custom_call_target="tpu_custom_call" | custom-call | tf_op jit(solution)/shard_map/pallas_call | solution.py:254
  66.4 0.0 copy-start
  66.4 1.7 %copy.11 = f32[128,384]{1,0:T(8,128)} copy(f32[128,384]{1,0:T(8,128)} %get-tuple-element.4) | data formatting | bytes 393216
  68.1 0.0 copy-done
  68.1 0.7 copy.12
Async XLA Ops:
  66.4 1.7 %copy-start = (f32[128,384]{1,0:T(8,128)S(1)}, f32[128,384]{1,0:T(8,128)}, u32[]{:S(2)}) copy-start(f32[128,384]{1,0:T(8,128)} %get-tuple-element.5) | copy-start | bytes 589828

commit v2 on v1

v2 whole, which is shorter than its diff:
```python
import functools

import jax
import jax.numpy as jnp
from jax import lax
from jax.experimental import pallas as pl
from jax.experimental.pallas import tpu as pltpu
from jax.sharding import PartitionSpec as P

MESH = pl.DeviceIdType.MESH
F32, BF16 = jnp.float32, jnp.bfloat16
X, Y, Z = 4, 4, 8
ROWS, WIDTH = 128, 384
HALF = WIDTH // 2

NEAR = [(0, 0), (1, 0), (3, 0), (0, 1), (0, 3), (2, 0), (0, 2), (1, 1)]
FAR = [(3, 3), (1, 3), (3, 1), (2, 1), (1, 2), (2, 3), (3, 2), (2, 2)]
LOW_AT = {slot: i for i, slot in enumerate(NEAR + FAR)}
HIGH_AT = {(dz, dc): 2 * i + dc for i, dz in enumerate((0, 1, 7, 2, 6, 3, 5, 4)) for dc in (0, 1)}
TAIL = 16
STEPS = 32767.0


def dot(a, b, over):
    return lax.dot_general(a, b, (over, ((), ())), preferred_element_type=F32)


def encode(ref, value):
    rows = value.shape[0]
    top = jnp.maximum(jnp.max(jnp.abs(value), axis=0, keepdims=True), 1e-30)
    exponent = jnp.ceil(jnp.log2(top))
    ref[0:rows, :] = jnp.round(value * (STEPS * jnp.exp2(-exponent))).astype(jnp.int32).astype(jnp.int16)
    ref[rows : rows + TAIL, :] = jnp.broadcast_to(exponent, (TAIL, value.shape[1])).astype(jnp.int32).astype(jnp.int16)


def decode(ref):
    rows = ref.shape[0] - TAIL
    exponent = ref[rows : rows + TAIL, :].astype(jnp.int32).astype(F32)[0:1]
    return ref[0:rows, :].astype(jnp.int32).astype(F32) * (jnp.exp2(exponent) * (1.0 / STEPS))


def kernel(
    low_in, high_in, partner_in, log_scale, bias_in,
    low_out, high_out,
    low, high, part, prow, weights, gl, gh,
    ship_a, ship_b, got_a, got_b, next_a, next_b, last_a, last_b,
    got_core, ship_three, ship_four, ship_two, ship_one, got_three, got_four, got_two, got_one,
    load_sems, send_sems, recv_sems,
):
    blk, narrow = lax.axis_index("blk"), lax.axis_index("narrow")
    x, z, y, core = blk // 16, (blk // 2) % 8, (narrow // 2) * 2 + blk % 2, narrow % 2

    def device(dx=0, dy=0, dz=0, dc=0):
        px, py, pz, pc = (x + dx) % X, (y + dy) % Y, (z + dz) % Z, (core + dc) % 2
        return ((px * Z + pz) * 2 + py % 2, (py // 2) * 2 + pc)

    copies = []

    def send(src, dst, **to):
        k = len(copies)
        copy = pltpu.make_async_remote_copy(
            src, dst, send_sems.at[k], recv_sems.at[k], device_id=device(**to), device_id_type=MESH
        )
        copy.start()
        copies.append(copy)
        return copy

    def low_rows(slot, first=0, count=ROWS):
        return pl.ds(LOW_AT[slot] * ROWS + first, count)

    def low_cols(slot):
        return pl.ds(LOW_AT[slot] * ROWS, ROWS)

    def high_rows(dz, dc, first=0, count=ROWS):
        return pl.ds(HIGH_AT[dz, dc] * ROWS + first, count)

    a_rows, b_rows = pl.ds(0, HALF), pl.ds(HALF, HALF)
    own_low, own_high = low.at[low_rows((0, 0))], high.at[high_rows(0, 0)]
    loads = [(low_in, own_low), (high_in, own_high), (partner_in, part.at[0, 0])]
    loads = [pltpu.make_async_copy(src, dst, load_sems.at[i]) for i, (src, dst) in enumerate(loads)]
    for load in loads:
        load.start()

    peers = [dict(dx=e) for e in (1, 2, 3)] + [dict(dy=e) for e in (1, 2, 3)]
    peers += [dict(dz=e) for e in (1, 2, 6, 7)] + [dict(dc=1)]
    barrier = pltpu.get_barrier_semaphore()
    for peer in peers:
        pl.semaphore_signal(barrier, inc=1, device_id=device(**peer), device_id_type=MESH)
    for load in loads:
        load.wait()
    scale = jnp.exp(jnp.full((1, 512), log_scale[0, 0], F32))
    gain, shift, half = 0.5 * scale, 0.5 * bias_in[0, 0], 0.5 * scale
    pl.semaphore_wait(barrier, len(peers))

    low_x, low_y, low_a, low_b, part_x, part_y, high_same, high_other = {}, {}, {}, {}, {}, {}, {}, {}
    for e in (1, 3):
        low_x[4 - e] = send(own_low, low.at[low_rows((4 - e, 0))], dx=e)
        low_y[4 - e] = send(own_low, low.at[low_rows((0, 4 - e))], dy=e)
    for e in (2, 6):
        high_same[8 - e] = send(own_high, high.at[high_rows(8 - e, 0)], dz=e)
    low_x[2] = send(own_low, low.at[low_rows((2, 0))], dx=2)
    low_y[2] = send(own_low, low.at[low_rows((0, 2))], dy=2)
    for e in (1, 7):
        high_same[8 - e] = send(own_high, high.at[high_rows(8 - e, 0)], dz=e)
    high_other[0] = send(own_high, high.at[high_rows(0, 1)], dc=1)
    for e in (1, 3, 2):
        part_x[4 - e] = send(part.at[0, 0], part.at[0, 4 - e], dx=e)

    def to_other_core(dz):
        rows = high_rows(dz, 0)
        high_other[dz] = send(high.at[rows], high.at[high_rows(dz, 1)], dc=1)

    def pass_low(d):
        low_x[d].wait_recv()
        for e in (1, 3, 2):
            src = low.at[low_rows((d, 0), 0, 64)]
            low_a[d, 4 - e] = send(src, low.at[low_rows((d, 4 - e), 0, 64)], dy=e)
        low_y[d].wait_recv()
        for e in (1, 3, 2):
            src = low.at[low_rows((0, d), 64, 64)]
            low_b[4 - e, d] = send(src, low.at[low_rows((4 - e, d), 64, 64)], dx=e)

    pass_low(1)
    pass_low(3)
    pass_low(2)
    high_same[6].wait_recv()
    high_same[5] = send(high.at[high_rows(6, 0)], high.at[high_rows(5, 0)], dz=1)
    four_a = send(high.at[high_rows(6, 0, 0, 64)], high.at[high_rows(4, 0, 0, 64)], dz=2)
    high_same[2].wait_recv()
    high_same[3] = send(high.at[high_rows(2, 0)], high.at[high_rows(3, 0)], dz=7)
    four_b = send(high.at[high_rows(2, 0, 64, 64)], high.at[high_rows(4, 0, 64, 64)], dz=6)
    for e in (1, 3, 2):
        part_x[e].wait_recv()
    for e in (1, 3, 2):
        part_y[4 - e] = send(part.at[0], part.at[4 - e], dy=e)
    for dz in (1, 7):
        high_same[dz].wait_recv()
        to_other_core(dz)
    to_other_core(2)
    to_other_core(6)

    started = set()

    def add_to(ref, index, keys, value):
        if keys <= started:
            ref[index] += value
        else:
            ref[index] = value
            started.update(keys)

    def block(low_slots, high_slots):
        first_low, first_high = LOW_AT[low_slots[0]], HIGH_AT[high_slots[0]]
        wide, tall = len(low_slots) * ROWS, len(high_slots) * ROWS
        cols, rows = pl.ds(first_low * ROWS, wide), pl.ds(first_high * ROWS, tall)
        low_block, high_block = low[cols, :], high[rows, :]
        logits = dot(high_block, low_block, ((1,), (1,)))
        wanted = prow[:, cols]
        for i, (dz, dc) in enumerate(high_slots):
            b, n = device(dz=dz, dc=dc)
            local = wanted - (b * 4 + n) * ROWS
            ids = lax.broadcasted_iota(jnp.int32, (ROWS, 512), 0)
            for left in range(0, wide, 512):
                here = (slice(i * ROWS, (i + 1) * ROWS), slice(left, left + 512))
                match = ids == local[:, left : left + 512]
                value = jnp.tanh(logits[here] * gain + shift) * half + jnp.where(match, -half, half)
                weights[here] = value.astype(BF16)
        w = weights[0:tall, 0:wide]
        add_to(gh, (rows, slice(None)), {("h", s) for s in high_slots}, dot(w, low_block, ((1,), (0,))))
        add_to(gl, (slice(None), cols), {("l", s) for s in low_slots}, dot(high_block, w, ((0,), (0,))))

    def take_part(slots):
        for dx, dy in slots:
            prow[:, low_cols((dx, dy))] = part[dy, dx]

    pairs = [[(dz, 0), (dz, 1)] for dz in (0, 1, 7, 2, 6, 3, 5, 4)]
    h_one, h_two, h_far = sum(pairs[:3], []), sum(pairs[3:5], []), sum(pairs[5:], [])

    for dz in (0, 1, 7):
        high_other[dz].wait_recv()
    low_a[1, 1].wait_recv()
    low_b[1, 1].wait_recv()
    for e in (1, 2, 3):
        part_y[e].wait_recv()
    take_part(NEAR + FAR)
    block(NEAR, h_one)
    for dz in (3, 5):
        high_same[dz].wait_recv()
        to_other_core(dz)
    for dz in (2, 6):
        high_other[dz].wait_recv()
    four_a.wait_recv()
    four_b.wait_recv()
    to_other_core(4)
    block(NEAR, h_two)
    for dz in (3, 5, 4):
        high_other[dz].wait_recv()
    block(NEAR, h_far)

    a_first, b_first, a_next, b_next = {}, {}, {}, {}

    def low_first(d, e):
        encode(ship_a.at[e, d], gl[a_rows, low_cols((d, e))])
        a_first[4 - e, d] = send(ship_a.at[e, d], got_a.at[4 - e, d], dy=e)
        encode(ship_b.at[e, d], gl[b_rows, low_cols((e, d))])
        b_first[4 - e, d] = send(ship_b.at[e, d], got_b.at[4 - e, d], dx=e)

    for e in (1, 3, 2):
        low_first(0, e)
    low_first(1, 1)
    for slot in FAR:
        low_a[slot].wait_recv()
        low_b[slot].wait_recv()
    block(FAR, h_far)

    from_core = {}

    def core_sum_send(dz):
        from_core[dz] = send(gh.at[high_rows(dz, 1)], got_core.at[dz], dc=1)

    def core_sum_take(dz):
        from_core[dz].wait_recv()
        gh[high_rows(dz, 0), :] += got_core[dz]

    for dz in (4, 3, 5):
        core_sum_send(dz)
    block(FAR[:4], h_one + h_two)
    core_sum_take(4)
    encode(ship_four.at[0], gh[high_rows(4, 0, 0, 64), :])
    encode(ship_four.at[1], gh[high_rows(4, 0, 64, 64), :])
    four_a = send(ship_four.at[0], got_four.at[0], dz=2)
    four_b = send(ship_four.at[1], got_four.at[1], dz=6)
    core_sum_take(3)
    core_sum_take(5)
    encode(ship_three.at[0], gh[high_rows(3, 0), :])
    encode(ship_three.at[1], gh[high_rows(5, 0), :])
    three_a = send(ship_three.at[0], got_three.at[0], dz=1)
    three_b = send(ship_three.at[1], got_three.at[1], dz=7)
    block(FAR[4:], h_one + h_two)
    for dz in (2, 6, 1, 7, 0):
        core_sum_send(dz)
    for d, e in ((1, 3), (3, 1), (3, 3), (2, 1), (1, 2), (2, 3), (3, 2), (2, 2)):
        low_first(d, e)

    for dz, i, three, four, first, to in ((2, 0, three_a, four_a, 0, 2), (6, 1, three_b, four_b, 64, 6)):
        core_sum_take(dz)
        three.wait_recv()
        four.wait_recv()
        gh[high_rows(dz, 0), :] += decode(got_three.at[i])
        gh[high_rows(dz, 0, first, 64), :] += decode(got_four.at[i])
        encode(ship_two.at[i], gh[high_rows(dz, 0), :])
        two = send(ship_two.at[i], got_two.at[i], dz=to)
        two_a, two_b = (two, None) if i == 0 else (two_a, two)
    core_sum_take(1)
    core_sum_take(7)
    encode(ship_one.at[0], gh[high_rows(1, 0), :])
    one_a = send(ship_one.at[0], got_one.at[0], dz=1)
    encode(ship_one.at[1], gh[high_rows(7, 0), :])
    one_b = send(ship_one.at[1], got_one.at[1], dz=7)

    for d in (1, 3, 2):
        for e in (1, 3, 2):
            a_first[e, d].wait_recv()
        total = gl[a_rows, low_cols((d, 0))]
        for e in (1, 2, 3):
            total += decode(got_a.at[e, d])
        encode(next_a.at[d], total)
        a_next[d] = send(next_a.at[d], last_a.at[d], dx=d)
        for e in (1, 3, 2):
            b_first[e, d].wait_recv()
        total = gl[b_rows, low_cols((0, d))]
        for e in (1, 2, 3):
            total += decode(got_b.at[e, d])
        encode(next_b.at[d], total)
        b_next[d] = send(next_b.at[d], last_b.at[d], dy=d)

    core_sum_take(0)
    for copy in (one_a, one_b, two_a, two_b):
        copy.wait_recv()
    total = gh[high_rows(0, 0), :] + decode(got_one.at[0]) + decode(got_one.at[1])
    high_out[...] = total + decode(got_two.at[0]) + decode(got_two.at[1])
    total_a, total_b = gl[a_rows, low_cols((0, 0))], gl[b_rows, low_cols((0, 0))]
    for e in (1, 3, 2):
        a_first[e, 0].wait_recv()
        b_first[e, 0].wait_recv()
        total_a += decode(got_a.at[e, 0])
        total_b += decode(got_b.at[e, 0])
    for d in (1, 3, 2):
        a_next[d].wait_recv()
        b_next[d].wait_recv()
        total_a += decode(last_a.at[d])
        total_b += decode(last_b.at[d])
    low_out[...] = jnp.concatenate([total_a, total_b], axis=0).T
    for copy in copies:
        copy.wait_send()


def per_device(embed_low, embed_high, partner, log_scale, bias):
    hbm, vmem, smem = (pl.BlockSpec(memory_space=m) for m in (pl.ANY, pltpu.VMEM, pltpu.SMEM))
    group = 16 * ROWS
    grad = jax.ShapeDtypeStruct((ROWS, WIDTH), F32)
    low_piece, high_piece = (HALF + TAIL, ROWS), (ROWS + TAIL, WIDTH)

    def short(*shape):
        return pltpu.VMEM(shape, jnp.int16)

    return pl.pallas_call(
        kernel,
        out_shape=(grad, grad),
        in_specs=[hbm, hbm, hbm, smem, smem],
        out_specs=(vmem, vmem),
        scratch_shapes=[
            pltpu.VMEM((group, WIDTH), BF16),
            pltpu.VMEM((group, WIDTH), BF16),
            pltpu.VMEM((4, 4, 1, ROWS), jnp.int32),
            pltpu.VMEM((1, group), jnp.int32),
            pltpu.VMEM((10 * ROWS, 8 * ROWS), BF16),
            pltpu.VMEM((WIDTH, group), F32),
            pltpu.VMEM((group, WIDTH), F32),
            short(4, 4, *low_piece),
            short(4, 4, *low_piece),
            short(4, 4, *low_piece),
            short(4, 4, *low_piece),
            short(4, *low_piece),
            short(4, *low_piece),
            short(4, *low_piece),
            short(4, *low_piece),
            pltpu.VMEM((8, ROWS, WIDTH), F32),
            short(2, *high_piece),
            short(2, ROWS // 2 + TAIL, WIDTH),
            short(2, *high_piece),
            short(2, *high_piece),
            short(2, *high_piece),
            short(2, ROWS // 2 + TAIL, WIDTH),
            short(2, *high_piece),
            short(2, *high_piece),
            pltpu.SemaphoreType.DMA((3,)),
            pltpu.SemaphoreType.DMA((96,)),
            pltpu.SemaphoreType.DMA((96,)),
        ],
        compiler_params=pltpu.CompilerParams(
            collective_id=0, has_side_effects=True, vmem_limit_bytes=56 * 2**20
        ),
    )(embed_low, embed_high, partner.reshape(1, ROWS), log_scale.reshape(1, 1), bias.reshape(1, 1))


def solution(mesh):
    in_specs = (
        P(("blk", "narrow"), None),
        P(("blk", "narrow"), None),
        P(("blk", "narrow")),
        P(),
        P(),
    )
    out_specs = (P(("blk", "narrow"), None), P(("blk", "narrow"), None))
    return jax.shard_map(
        per_device, mesh=mesh, in_specs=in_specs, out_specs=out_specs, check_vma=False
    )
```

time: 68.9 us -> 58.3 us (0.85)
  Pallas kernels: 63.8 us -> 53.9 us
    pallas_call x1, Pallas kernels: 63.8 us -> 53.9 us  [per_device(): pl.pallas_call(kernel, out_shape=(grad, grad), in_specs=[hbm, hbm, hbm, s...]
where the time goes in v2:
time: 58.3 us; the launch traced here: 58.1 us
  Pallas kernels  53.9 us (92%)
  local copies, waits for them, and re-layouts  2.34 us (4%)
  between operations  1.94 us (3%)
    pallas_call x1, Pallas kernels, per_device(): pl.pallas_call(kernel, out_shape=(grad, grad), in_specs=[hbm, hbm, hbm, s...  53.9 us
    unnamed x4, local copies, waits for them, and re-layouts  2.34 us

profile of v2, /device:TPU:1, one launch (start us, length us, event | category | flops | bytes accessed | tf_op | source)
XLA Modules:
  0.0 58.1 jit_solution(11662910915912160841)
XLA Ops:
  1.9 53.9 %shard_map.68 = (f32[128,384]{1,0:T(8,128)}, f32[128,384]{1,0:T(8,128)}) custom-call(bf16[128,384]{1,0:T(8,128)(2,1)} %low_in.1, bf16[128,384]{1,0:T(8,128)(2,1)} %high_in.1, s32[1,128]{1,0:T(1,128)} %bitcast.5, f32[1,1]{1,0:T(1,128)} %bitcast.3.log_scale, f32[1,1]{1,0:T(1,128)} %bitcast.4.bias_in), custom_call_target="tpu_custom_call" | custom-call | tf_op jit(solution)/shard_map/pallas_call | solution.py:306
  55.8 0.0 copy-start
  55.8 1.7 %copy.11 = f32[128,384]{1,0:T(8,128)} copy(f32[128,384]{1,0:T(8,128)} %get-tuple-element.4) | data formatting | bytes 393216
  57.5 0.0 copy-done
  57.5 0.7 %copy.12 = f32[128,384]{1,0:T(8,128)} copy(f32[128,384]{1,0:T(8,128)S(1)} %copy-done) | data formatting | bytes 393216
Async XLA Ops:
  55.8 1.7 %copy-start = (f32[128,384]{1,0:T(8,128)S(1)}, f32[128,384]{1,0:T(8,128)}, u32[]{:S(2)}) copy-start(f32[128,384]{1,0:T(8,128)} %get-tuple-element.5) | copy-start | bytes 589828

commit v3 on v2

--- a/solution.py
+++ b/solution.py
@@ -16,7 +16,9 @@
 NEAR = [(0, 0), (1, 0), (3, 0), (0, 1), (0, 3), (2, 0), (0, 2), (1, 1)]
 FAR = [(3, 3), (1, 3), (3, 1), (2, 1), (1, 2), (2, 3), (3, 2), (2, 2)]
 LOW_AT = {slot: i for i, slot in enumerate(NEAR + FAR)}
-HIGH_AT = {(dz, dc): 2 * i + dc for i, dz in enumerate((0, 1, 7, 2, 6, 3, 5, 4)) for dc in (0, 1)}
+HIGH_NEAR = [(0, 0), (0, 1), (1, 0), (7, 0), (1, 1), (7, 1), (6, 0), (2, 0), (6, 1), (2, 1)]
+HIGH_FAR = [(4, 0), (4, 1), (3, 0), (3, 1), (5, 0), (5, 1)]
+HIGH_AT = {slot: i for i, slot in enumerate(HIGH_NEAR + HIGH_FAR)}
 TAIL = 16
 STEPS = 32767.0
 
@@ -74,6 +76,9 @@
     def high_rows(dz, dc, first=0, count=ROWS):
         return pl.ds(HIGH_AT[dz, dc] * ROWS + first, count)
 
+    def high_cols(dz, dc):
+        return pl.ds(HIGH_AT[dz, dc] * ROWS, ROWS)
+
     a_rows, b_rows = pl.ds(0, HALF), pl.ds(HALF, HALF)
     own_low, own_high = low.at[low_rows((0, 0))], high.at[high_rows(0, 0)]
     loads = [(low_in, own_low), (high_in, own_high), (partner_in, part.at[0, 0])]
@@ -93,6 +98,8 @@
     pl.semaphore_wait(barrier, len(peers))
 
     low_x, low_y, low_a, low_b, part_x, part_y, high_same, high_other = {}, {}, {}, {}, {}, {}, {}, {}
+    for e in (1, 3, 2):
+        part_x[4 - e] = send(part.at[0, 0], part.at[0, 4 - e], dx=e)
     for e in (1, 3):
         low_x[4 - e] = send(own_low, low.at[low_rows((4 - e, 0))], dx=e)
         low_y[4 - e] = send(own_low, low.at[low_rows((0, 4 - e))], dy=e)
@@ -103,8 +110,6 @@
     for e in (1, 7):
         high_same[8 - e] = send(own_high, high.at[high_rows(8 - e, 0)], dz=e)
     high_other[0] = send(own_high, high.at[high_rows(0, 1)], dc=1)
-    for e in (1, 3, 2):
-        part_x[4 - e] = send(part.at[0, 0], part.at[0, 4 - e], dx=e)
 
     def to_other_core(dz):
         rows = high_rows(dz, 0)
@@ -120,6 +125,10 @@
             src = low.at[low_rows((0, d), 64, 64)]
             low_b[4 - e, d] = send(src, low.at[low_rows((4 - e, d), 64, 64)], dx=e)
 
+    for e in (1, 3, 2):
+        part_x[e].wait_recv()
+    for e in (1, 3, 2):
+        part_y[4 - e] = send(part.at[0], part.at[4 - e], dy=e)
     pass_low(1)
     pass_low(3)
     pass_low(2)
@@ -129,15 +138,11 @@
     high_same[2].wait_recv()
     high_same[3] = send(high.at[high_rows(2, 0)], high.at[high_rows(3, 0)], dz=7)
     four_b = send(high.at[high_rows(2, 0, 64, 64)], high.at[high_rows(4, 0, 64, 64)], dz=6)
-    for e in (1, 3, 2):
-        part_x[e].wait_recv()
-    for e in (1, 3, 2):
-        part_y[4 - e] = send(part.at[0], part.at[4 - e], dy=e)
     for dz in (1, 7):
         high_same[dz].wait_recv()
         to_other_core(dz)
+    to_other_core(6)
     to_other_core(2)
-    to_other_core(6)
 
     started = set()
 
@@ -165,98 +170,112 @@
                 value = jnp.tanh(logits[here] * gain + shift) * half + jnp.where(match, -half, half)
                 weights[here] = value.astype(BF16)
         w = weights[0:tall, 0:wide]
-        add_to(gh, (rows, slice(None)), {("h", s) for s in high_slots}, dot(w, low_block, ((1,), (0,))))
+        add_to(gh, (slice(None), rows), {("h", s) for s in high_slots}, dot(low_block, w, ((0,), (1,))))
         add_to(gl, (slice(None), cols), {("l", s) for s in low_slots}, dot(high_block, w, ((0,), (0,))))
 
     def take_part(slots):
         for dx, dy in slots:
             prow[:, low_cols((dx, dy))] = part[dy, dx]
 
-    pairs = [[(dz, 0), (dz, 1)] for dz in (0, 1, 7, 2, 6, 3, 5, 4)]
-    h_one, h_two, h_far = sum(pairs[:3], []), sum(pairs[3:5], []), sum(pairs[5:], [])
-
-    for dz in (0, 1, 7):
-        high_other[dz].wait_recv()
+    a_first, b_first, a_next, b_next = {}, {}, {}, {}
+
+    def low_first(slots):
+        for dx, dy in slots:
+            if dy:
+                encode(ship_a.at[dy, dx], gl[a_rows, low_cols((dx, dy))])
+            if dx:
+                encode(ship_b.at[dx, dy], gl[b_rows, low_cols((dx, dy))])
+        for dx, dy in slots:
+            if dy:
+                a_first[4 - dy, dx] = send(ship_a.at[dy, dx], got_a.at[4 - dy, dx], dy=dy)
+            if dx:
+                b_first[4 - dx, dy] = send(ship_b.at[dx, dy], got_b.at[4 - dx, dy], dx=dx)
+
+    from_core = {}
+
+    def core_sum_send(dz):
+        from_core[dz] = send(gh.at[:, high_cols(dz, 1)], got_core.at[dz], dc=1)
+
+    def core_sum_take(dz):
+        from_core[dz].wait_recv()
+        gh[:, high_cols(dz, 0)] += got_core[dz]
+
     low_a[1, 1].wait_recv()
     low_b[1, 1].wait_recv()
     for e in (1, 2, 3):
         part_y[e].wait_recv()
     take_part(NEAR + FAR)
-    block(NEAR, h_one)
+    high_other[0].wait_recv()
+    block(NEAR, HIGH_NEAR[:4])
+    for dz in (1, 7, 6, 2):
+        high_other[dz].wait_recv()
+    block(NEAR, HIGH_NEAR[4:])
+    for slot in FAR[:4]:
+        low_a[slot].wait_recv()
+        low_b[slot].wait_recv()
+    block(FAR[:4], HIGH_NEAR[:4])
     for dz in (3, 5):
         high_same[dz].wait_recv()
         to_other_core(dz)
-    for dz in (2, 6):
-        high_other[dz].wait_recv()
     four_a.wait_recv()
     four_b.wait_recv()
     to_other_core(4)
-    block(NEAR, h_two)
-    for dz in (3, 5, 4):
-        high_other[dz].wait_recv()
-    block(NEAR, h_far)
-
-    a_first, b_first, a_next, b_next = {}, {}, {}, {}
-
-    def low_first(d, e):
-        encode(ship_a.at[e, d], gl[a_rows, low_cols((d, e))])
-        a_first[4 - e, d] = send(ship_a.at[e, d], got_a.at[4 - e, d], dy=e)
-        encode(ship_b.at[e, d], gl[b_rows, low_cols((e, d))])
-        b_first[4 - e, d] = send(ship_b.at[e, d], got_b.at[4 - e, d], dx=e)
-
-    for e in (1, 3, 2):
-        low_first(0, e)
-    low_first(1, 1)
-    for slot in FAR:
+    block(FAR[:4], HIGH_NEAR[4:])
+    for slot in FAR[4:]:
         low_a[slot].wait_recv()
         low_b[slot].wait_recv()
-    block(FAR, h_far)
-
-    from_core = {}
-
-    def core_sum_send(dz):
-        from_core[dz] = send(gh.at[high_rows(dz, 1)], got_core.at[dz], dc=1)
-
-    def core_sum_take(dz):
-        from_core[dz].wait_recv()
-        gh[high_rows(dz, 0), :] += got_core[dz]
-
-    for dz in (4, 3, 5):
+    block(FAR[4:], HIGH_NEAR[:6])
+    for dz in (1, 7, 0):
         core_sum_send(dz)
-    block(FAR[:4], h_one + h_two)
+    high_other[4].wait_recv()
+    high_other[3].wait_recv()
+    block(NEAR, HIGH_FAR[:4])
+    core_sum_take(1)
+    core_sum_take(7)
+    encode(ship_one.at[0], gh[:, high_cols(1, 0)])
+    encode(ship_one.at[1], gh[:, high_cols(7, 0)])
+    one_a = send(ship_one.at[0], got_one.at[0], dz=1)
+    one_b = send(ship_one.at[1], got_one.at[1], dz=7)
+    block(FAR, HIGH_FAR[:4])
+    core_sum_send(4)
+    core_sum_send(3)
+    high_other[5].wait_recv()
+    block(FAR[:4], HIGH_FAR[4:])
+    low_first(FAR[:4])
+    block(NEAR, HIGH_FAR[4:])
     core_sum_take(4)
-    encode(ship_four.at[0], gh[high_rows(4, 0, 0, 64), :])
-    encode(ship_four.at[1], gh[high_rows(4, 0, 64, 64), :])
+    core_sum_take(3)
+    encode(ship_four.at[0], gh[a_rows, high_cols(4, 0)])
+    encode(ship_four.at[1], gh[b_rows, high_cols(4, 0)])
+    encode(ship_three.at[0], gh[:, high_cols(3, 0)])
     four_a = send(ship_four.at[0], got_four.at[0], dz=2)
     four_b = send(ship_four.at[1], got_four.at[1], dz=6)
-    core_sum_take(3)
+    three_a = send(ship_three.at[0], got_three.at[0], dz=1)
+    low_first(NEAR)
+    block(FAR[4:], HIGH_FAR[4:])
+    core_sum_send(5)
+    block(FAR[4:], HIGH_NEAR[6:])
+    core_sum_send(6)
+    core_sum_send(2)
+    low_first(FAR[4:])
     core_sum_take(5)
-    encode(ship_three.at[0], gh[high_rows(3, 0), :])
-    encode(ship_three.at[1], gh[high_rows(5, 0), :])
-    three_a = send(ship_three.at[0], got_three.at[0], dz=1)
+    encode(ship_three.at[1], gh[:, high_cols(5, 0)])
     three_b = send(ship_three.at[1], got_three.at[1], dz=7)
-    block(FAR[4:], h_one + h_two)
-    for dz in (2, 6, 1, 7, 0):
-        core_sum_send(dz)
-    for d, e in ((1, 3), (3, 1), (3, 3), (2, 1), (1, 2), (2, 3), (3, 2), (2, 2)):
-        low_first(d, e)
-
-    for dz, i, three, four, first, to in ((2, 0, three_a, four_a, 0, 2), (6, 1, three_b, four_b, 64, 6)):
-        core_sum_take(dz)
-        three.wait_recv()
-        four.wait_recv()
-        gh[high_rows(dz, 0), :] += decode(got_three.at[i])
-        gh[high_rows(dz, 0, first, 64), :] += decode(got_four.at[i])
-        encode(ship_two.at[i], gh[high_rows(dz, 0), :])
-        two = send(ship_two.at[i], got_two.at[i], dz=to)
-        two_a, two_b = (two, None) if i == 0 else (two_a, two)
-    core_sum_take(1)
-    core_sum_take(7)
-    encode(ship_one.at[0], gh[high_rows(1, 0), :])
-    one_a = send(ship_one.at[0], got_one.at[0], dz=1)
-    encode(ship_one.at[1], gh[high_rows(7, 0), :])
-    one_b = send(ship_one.at[1], got_one.at[1], dz=7)
-
+
+    core_sum_take(2)
+    core_sum_take(6)
+    three_a.wait_recv()
+    four_a.wait_recv()
+    gh[:, high_cols(2, 0)] += decode(got_three.at[0])
+    gh[a_rows, high_cols(2, 0)] += decode(got_four.at[0])
+    encode(ship_two.at[0], gh[:, high_cols(2, 0)])
+    two_a = send(ship_two.at[0], got_two.at[0], dz=2)
+    three_b.wait_recv()
+    four_b.wait_recv()
+    gh[:, high_cols(6, 0)] += decode(got_three.at[1])
+    gh[b_rows, high_cols(6, 0)] += decode(got_four.at[1])
+    encode(ship_two.at[1], gh[:, high_cols(6, 0)])
+    two_b = send(ship_two.at[1], got_two.at[1], dz=6)
     for d in (1, 3, 2):
         for e in (1, 3, 2):
             a_first[e, d].wait_recv()
@@ -276,8 +295,8 @@
     core_sum_take(0)
     for copy in (one_a, one_b, two_a, two_b):
         copy.wait_recv()
-    total = gh[high_rows(0, 0), :] + decode(got_one.at[0]) + decode(got_one.at[1])
-    high_out[...] = total + decode(got_two.at[0]) + decode(got_two.at[1])
+    total = gh[:, high_cols(0, 0)] + decode(got_one.at[0]) + decode(got_one.at[1])
+    high_out[...] = (total + decode(got_two.at[0]) + decode(got_two.at[1])).T
     total_a, total_b = gl[a_rows, low_cols((0, 0))], gl[b_rows, low_cols((0, 0))]
     for e in (1, 3, 2):
         a_first[e, 0].wait_recv()
@@ -298,7 +317,7 @@
     hbm, vmem, smem = (pl.BlockSpec(memory_space=m) for m in (pl.ANY, pltpu.VMEM, pltpu.SMEM))
     group = 16 * ROWS
     grad = jax.ShapeDtypeStruct((ROWS, WIDTH), F32)
-    low_piece, high_piece = (HALF + TAIL, ROWS), (ROWS + TAIL, WIDTH)
+    half_piece, piece = (HALF + TAIL, ROWS), (WIDTH + TAIL, ROWS)
 
     def short(*shape):
         return pltpu.VMEM(shape, jnp.int16)
@@ -313,26 +332,26 @@
             pltpu.VMEM((group, WIDTH), BF16),
             pltpu.VMEM((4, 4, 1, ROWS), jnp.int32),
             pltpu.VMEM((1, group), jnp.int32),
-            pltpu.VMEM((10 * ROWS, 8 * ROWS), BF16),
+            pltpu.VMEM((8 * ROWS, 8 * ROWS), BF16),
             pltpu.VMEM((WIDTH, group), F32),
-            pltpu.VMEM((group, WIDTH), F32),
-            short(4, 4, *low_piece),
-            short(4, 4, *low_piece),
-            short(4, 4, *low_piece),
-            short(4, 4, *low_piece),
-            short(4, *low_piece),
-            short(4, *low_piece),
-            short(4, *low_piece),
-            short(4, *low_piece),
-            pltpu.VMEM((8, ROWS, WIDTH), F32),
-            short(2, *high_piece),
-            short(2, ROWS // 2 + TAIL, WIDTH),
-            short(2, *high_piece),
-            short(2, *high_piece),
-            short(2, *high_piece),
-            short(2, ROWS // 2 + TAIL, WIDTH),
-            short(2, *high_piece),
-            short(2, *high_piece),
+            pltpu.VMEM((WIDTH, group), F32),
+            short(4, 4, *half_piece),
+            short(4, 4, *half_piece),
+            short(4, 4, *half_piece),
+            short(4, 4, *half_piece),
+            short(4, *half_piece),
+            short(4, *half_piece),
+            short(4, *half_piece),
+            short(4, *half_piece),
+            pltpu.VMEM((8, WIDTH, ROWS), F32),
+            short(2, *piece),
+            short(2, *half_piece),
+            short(2, *piece),
+            short(2, *piece),
+            short(2, *piece),
+            short(2, *half_piece),
+            short(2, *piece),
+            short(2, *piece),
             pltpu.SemaphoreType.DMA((3,)),
             pltpu.SemaphoreType.DMA((96,)),
             pltpu.SemaphoreType.DMA((96,)),

time: 58.3 us -> 55.3 us (0.949)
  Pallas kernels: 53.9 us -> 50.6 us
    pallas_call x1, Pallas kernels: 53.9 us -> 50.6 us  [per_device(): pl.pallas_call(kernel, out_shape=(grad, grad), in_specs=[hbm, hbm, hbm, s...]
where the time goes in v3:
time: 55.3 us; the launch traced here: 54.9 us
  Pallas kernels  50.6 us (92%)
  local copies, waits for them, and re-layouts  2.34 us (4%)
  between operations  1.94 us (4%)
    pallas_call x1, Pallas kernels, per_device(): pl.pallas_call(kernel, out_shape=(grad, grad), in_specs=[hbm, hbm, hbm, s...  50.6 us
    unnamed x4, local copies, waits for them, and re-layouts  2.34 us

profile of v3, /device:TPU:1, one launch (start us, length us, event | category | flops | bytes accessed | tf_op | source)
XLA Modules:
  0.0 54.9 jit_solution(7173987281390472088)
XLA Ops:
  1.9 50.6 %shard_map.68 = (f32[128,384]{1,0:T(8,128)}, f32[128,384]{1,0:T(8,128)}) custom-call(bf16[128,384]{1,0:T(8,128)(2,1)} %low_in.1, bf16[128,384]{1,0:T(8,128)(2,1)} %high_in.1, s32[1,128]{1,0:T(1,128)} %bitcast.5, f32[1,1]{1,0:T(1,128)} %bitcast.3.log_scale, f32[1,1]{1,0:T(1,128)} %bitcast.4.bias_in), custom_call_target="tpu_custom_call" | custom-call | tf_op jit(solution)/shard_map/pallas_call | solution.py:325
  52.6 0.0 copy-start
  52.6 1.7 %copy.11 = f32[128,384]{1,0:T(8,128)} copy(f32[128,384]{1,0:T(8,128)} %get-tuple-element.4) | data formatting | bytes 393216
  54.2 0.0 copy-done
  54.2 0.7 %copy.12 = f32[128,384]{1,0:T(8,128)} copy(f32[128,384]{1,0:T(8,128)S(1)} %copy-done) | data formatting | bytes 393216
Async XLA Ops:
  52.6 1.7 %copy-start = (f32[128,384]{1,0:T(8,128)S(1)}, f32[128,384]{1,0:T(8,128)}, u32[]{:S(2)}) copy-start(f32[128,384]{1,0:T(8,128)} %get-tuple-element.5) | copy-start | bytes 589828

commit v4 on v3

--- a/solution.py
+++ b/solution.py
@@ -43,7 +43,7 @@
 
 def kernel(
     low_in, high_in, partner_in, log_scale, bias_in,
-    low_out, high_out,
+    out,
     low, high, part, prow, weights, gl, gh,
     ship_a, ship_b, got_a, got_b, next_a, next_b, last_a, last_b,
     got_core, ship_three, ship_four, ship_two, ship_one, got_three, got_four, got_two, got_one,
@@ -293,22 +293,24 @@
         b_next[d] = send(next_b.at[d], last_b.at[d], dy=d)
 
     core_sum_take(0)
-    for copy in (one_a, one_b, two_a, two_b):
-        copy.wait_recv()
+    one_a.wait_recv()
+    one_b.wait_recv()
     total = gh[:, high_cols(0, 0)] + decode(got_one.at[0]) + decode(got_one.at[1])
-    high_out[...] = (total + decode(got_two.at[0]) + decode(got_two.at[1])).T
     total_a, total_b = gl[a_rows, low_cols((0, 0))], gl[b_rows, low_cols((0, 0))]
     for e in (1, 3, 2):
         a_first[e, 0].wait_recv()
         b_first[e, 0].wait_recv()
         total_a += decode(got_a.at[e, 0])
         total_b += decode(got_b.at[e, 0])
+    two_a.wait_recv()
+    two_b.wait_recv()
+    out[ROWS:, :] = (total + decode(got_two.at[0]) + decode(got_two.at[1])).T
     for d in (1, 3, 2):
         a_next[d].wait_recv()
         b_next[d].wait_recv()
         total_a += decode(last_a.at[d])
         total_b += decode(last_b.at[d])
-    low_out[...] = jnp.concatenate([total_a, total_b], axis=0).T
+    out[:ROWS, :] = jnp.concatenate([total_a, total_b], axis=0).T
     for copy in copies:
         copy.wait_send()
 
@@ -316,17 +318,17 @@
 def per_device(embed_low, embed_high, partner, log_scale, bias):
     hbm, vmem, smem = (pl.BlockSpec(memory_space=m) for m in (pl.ANY, pltpu.VMEM, pltpu.SMEM))
     group = 16 * ROWS
-    grad = jax.ShapeDtypeStruct((ROWS, WIDTH), F32)
+    grads = jax.ShapeDtypeStruct((2 * ROWS, WIDTH), F32)
     half_piece, piece = (HALF + TAIL, ROWS), (WIDTH + TAIL, ROWS)
 
     def short(*shape):
         return pltpu.VMEM(shape, jnp.int16)
 
-    return pl.pallas_call(
+    grads = pl.pallas_call(
         kernel,
-        out_shape=(grad, grad),
+        out_shape=grads,
         in_specs=[hbm, hbm, hbm, smem, smem],
-        out_specs=(vmem, vmem),
+        out_specs=vmem,
         scratch_shapes=[
             pltpu.VMEM((group, WIDTH), BF16),
             pltpu.VMEM((group, WIDTH), BF16),
@@ -360,6 +362,7 @@
             collective_id=0, has_side_effects=True, vmem_limit_bytes=56 * 2**20
         ),
     )(embed_low, embed_high, partner.reshape(1, ROWS), log_scale.reshape(1, 1), bias.reshape(1, 1))
+    return grads[:ROWS], grads[ROWS:]
 
 
 def solution(mesh):

time: 55.3 us -> 54.7 us (0.989)
    unnamed x4 -> x0, local copies, waits for them, and re-layouts: 2.34 us -> none
    slice x0 -> x1, local copies, waits for them, and re-layouts: none -> 1.79 us  [per_device(): return (grads[:ROWS], grads[ROWS:])]
where the time goes in v4:
time: 54.7 us; the launch traced here: 54.3 us
  Pallas kernels  50.6 us (93%)
  between operations  1.93 us (4%)
  local copies, waits for them, and re-layouts  1.79 us (3%)
    pallas_call x1, Pallas kernels, per_device(): pl.pallas_call(kernel, out_shape=grads, in_specs=[hbm, hbm, hbm, smem, sm...  50.6 us
    slice x1, local copies, waits for them, and re-layouts, per_device(): return (grads[:ROWS], grads[ROWS:])  1.79 us

profile of v4, /device:TPU:1, one launch (start us, length us, event | category | flops | bytes accessed | tf_op | source)
XLA Modules:
  0.0 54.3 jit_solution(9864752096838819029)
XLA Ops:
  1.9 50.6 %shard_map.68 = f32[256,384]{1,0:T(8,128)} custom-call(bf16[128,384]{1,0:T(8,128)(2,1)} %low_in.1, bf16[128,384]{1,0:T(8,128)(2,1)} %high_in.1, s32[1,128]{1,0:T(1,128)} %bitcast.5, f32[1,1]{1,0:T(1,128)} %bitcast.3.log_scale, f32[1,1]{1,0:T(1,128)} %bitcast.4.bias_in), custom_call_target="tpu_custom_call" | custom-call | tf_op jit(solution)/shard_map/pallas_call | solution.py:327
  52.5 1.8 %fusion = (f32[128,384]{1,0:T(8,128)}, f32[128,384]{1,0:T(8,128)}) fusion(f32[256,384]{1,0:T(8,128)} %shard_map.68), kind=kLoop, calls=%fused_computation | loop fusion | bytes 786432 | tf_op jit(solution)/shard_map/slice | solution.py:365

commit v5 on v4

--- a/solution.py
+++ b/solution.py
@@ -83,14 +83,14 @@
     own_low, own_high = low.at[low_rows((0, 0))], high.at[high_rows(0, 0)]
     loads = [(low_in, own_low), (high_in, own_high), (partner_in, part.at[0, 0])]
     loads = [pltpu.make_async_copy(src, dst, load_sems.at[i]) for i, (src, dst) in enumerate(loads)]
-    for load in loads:
-        load.start()
 
     peers = [dict(dx=e) for e in (1, 2, 3)] + [dict(dy=e) for e in (1, 2, 3)]
     peers += [dict(dz=e) for e in (1, 2, 6, 7)] + [dict(dc=1)]
     barrier = pltpu.get_barrier_semaphore()
     for peer in peers:
         pl.semaphore_signal(barrier, inc=1, device_id=device(**peer), device_id_type=MESH)
+    for load in loads:
+        load.start()
     for load in loads:
         load.wait()
     scale = jnp.exp(jnp.full((1, 512), log_scale[0, 0], F32))
@@ -131,13 +131,13 @@
         part_y[4 - e] = send(part.at[0], part.at[4 - e], dy=e)
     pass_low(1)
     pass_low(3)
-    pass_low(2)
     high_same[6].wait_recv()
     high_same[5] = send(high.at[high_rows(6, 0)], high.at[high_rows(5, 0)], dz=1)
     four_a = send(high.at[high_rows(6, 0, 0, 64)], high.at[high_rows(4, 0, 0, 64)], dz=2)
     high_same[2].wait_recv()
     high_same[3] = send(high.at[high_rows(2, 0)], high.at[high_rows(3, 0)], dz=7)
     four_b = send(high.at[high_rows(2, 0, 64, 64)], high.at[high_rows(4, 0, 64, 64)], dz=6)
+    pass_low(2)
     for dz in (1, 7):
         high_same[dz].wait_recv()
         to_other_core(dz)
@@ -200,13 +200,14 @@
         from_core[dz].wait_recv()
         gh[:, high_cols(dz, 0)] += got_core[dz]
 
-    low_a[1, 1].wait_recv()
-    low_b[1, 1].wait_recv()
     for e in (1, 2, 3):
         part_y[e].wait_recv()
     take_part(NEAR + FAR)
     high_other[0].wait_recv()
-    block(NEAR, HIGH_NEAR[:4])
+    block(NEAR[:4], HIGH_NEAR[:4])
+    low_a[1, 1].wait_recv()
+    low_b[1, 1].wait_recv()
+    block(NEAR[4:], HIGH_NEAR[:4])
     for dz in (1, 7, 6, 2):
         high_other[dz].wait_recv()
     block(NEAR, HIGH_NEAR[4:])
@@ -230,15 +231,15 @@
     high_other[4].wait_recv()
     high_other[3].wait_recv()
     block(NEAR, HIGH_FAR[:4])
+    block(FAR, HIGH_FAR[:4])
+    core_sum_send(4)
+    core_sum_send(3)
     core_sum_take(1)
     core_sum_take(7)
     encode(ship_one.at[0], gh[:, high_cols(1, 0)])
     encode(ship_one.at[1], gh[:, high_cols(7, 0)])
     one_a = send(ship_one.at[0], got_one.at[0], dz=1)
     one_b = send(ship_one.at[1], got_one.at[1], dz=7)
-    block(FAR, HIGH_FAR[:4])
-    core_sum_send(4)
-    core_sum_send(3)
     high_other[5].wait_recv()
     block(FAR[:4], HIGH_FAR[4:])
     low_first(FAR[:4])

time: 54.7 us -> 54 us (0.987)
  Pallas kernels: 50.6 us -> 49.9 us
    pallas_call x1, Pallas kernels: 50.6 us -> 49.9 us  [per_device(): pl.pallas_call(kernel, out_shape=grads, in_specs=[hbm, hbm, hbm, smem, sm...]
where the time goes in v5:
time: 54 us; the launch traced here: 53.7 us
  Pallas kernels  49.9 us (92%)
  between operations  1.93 us (4%)
  local copies, waits for them, and re-layouts  1.79 us (3%)
    pallas_call x1, Pallas kernels, per_device(): pl.pallas_call(kernel, out_shape=grads, in_specs=[hbm, hbm, hbm, smem, sm...  49.9 us
    slice x1, local copies, waits for them, and re-layouts, per_device(): return (grads[:ROWS], grads[ROWS:])  1.79 us

profile of v5, /device:TPU:1, one launch (start us, length us, event | category | flops | bytes accessed | tf_op | source)
XLA Modules:
  0.0 53.7 jit_solution(9060465454602357218)
XLA Ops:
  1.9 49.9 %shard_map.68 = f32[256,384]{1,0:T(8,128)} custom-call(bf16[128,384]{1,0:T(8,128)(2,1)} %low_in.1, bf16[128,384]{1,0:T(8,128)(2,1)} %high_in.1, s32[1,128]{1,0:T(1,128)} %bitcast.5, f32[1,1]{1,0:T(1,128)} %bitcast.3.log_scale, f32[1,1]{1,0:T(1,128)} %bitcast.4.bias_in), custom_call_target="tpu_custom_call" | custom-call | tf_op jit(solution)/shard_map/pallas_call | solution.py:328
  51.9 1.8 %fusion = (f32[128,384]{1,0:T(8,128)}, f32[128,384]{1,0:T(8,128)}) fusion(f32[256,384]{1,0:T(8,128)} %shard_map.68), kind=kLoop, calls=%fused_computation | loop fusion | bytes 786432 | tf_op jit(solution)/shard_map/slice | solution.py:366
